TPU v7x, 128 devices: a whole 4x4x4 slice. The times are simulated.
128 devices in a mesh: lat: 8 (over y, core), lon: 16 (over x, z).
Axes of the slice: x: 4, y: 4, z: 4, core: 2. Of those that a mesh axis runs over, the one named last changes fastest.
Arguments:
- grid_nodes: bfloat16 [128, 1024, 512], P('lat', 'lon'), may hold values from -6 to 6
- mesh_nodes: bfloat16 [65536, 512], P(('lat', 'lon')), may hold values from -6 to 6
- g2m_edges: bfloat16 [1792, 128, 512], P(('lat', 'lon')), may hold values from -6 to 6
- mesh_edges: bfloat16 [2048, 128, 512], P(('lat', 'lon')), may hold values from -6 to 6
- g2m_sender: int32 [1792, 128], P(('lat', 'lon')), may hold values from 0 to 1727, as said below
- g2m_receiver: int32 [1792, 128], P(('lat', 'lon')), may hold values from -1 to 127, as said below
- g2m_window: int32 [1792], P(('lat', 'lon')), may hold values from 0 to 3, as said below
- mesh_sender: int32 [2048, 128], P(('lat', 'lon')), may hold values from 0 to 4287, as said below
- mesh_receiver: int32 [2048, 128], P(('lat', 'lon')), may hold values from -1 to 127, as said below
- mesh_window: int32 [2048], P(('lat', 'lon')), may hold values from 0 to 3, as said below
- near_rows: int32 [128, 9, 192], P(('lat', 'lon')), may hold values from -1 to 511, as said below
- far_rows: int32 [128, 128, 16], P(('lat', 'lon')), may hold values from -1 to 511, as said below
- w_g2m_edge: bfloat16 [4, 512, 512], replicated, may hold values from -0.25 to 0.25
- w_mesh_node: bfloat16 [3, 512, 512], replicated, may hold values from -0.25 to 0.25
- w_grid_node: bfloat16 [2, 512, 512], replicated, may hold values from -0.25 to 0.25
- w_proc_edge: bfloat16 [4, 512, 512], replicated, may hold values from -0.25 to 0.25
- w_proc_node: bfloat16 [3, 512, 512], replicated, may hold values from -0.25 to 0.25
- norms: float32 [5, 2, 512], replicated, may hold values from 0.1 to 1.9
Outputs:
- mesh_out: bfloat16 [65536, 512], P(('lat', 'lon'))
- grid_out: bfloat16 [128, 1024, 512], P('lat', 'lon')
Inputs may be any that keep to these rules, and one draw needn't show every extreme that they name: `g2m_sender`: flat index i * 72 + j of a cell of the owning device's grid block extended by 4 cells on every side; no edge names a cell above the first or below the last grid row. `g2m_receiver`: position of the receiving mesh node in the block's window of 128 of the device's mesh nodes; -1 marks an empty slot. `g2m_window`: window of 128 of the device's own mesh nodes that holds the block's receivers. `mesh_sender`: below 512: one of the device's own mesh nodes. From 512 to 2239: slot s of the list that the neighbouring patch at relative position q sends to this device, and that patch exists and the slot is live. Above: slot s of the list that device p sends to this device, and that slot is live. Every device's edges read the first slot of every other device's list to it. `mesh_receiver`: position of the receiving mesh node in the block's window of 128 of the device's mesh nodes; -1 marks an empty slot. `mesh_window`: window of 128 of the device's own mesh nodes that holds the block's receivers. `near_rows`: entry [p, q] lists own mesh nodes of device p sent to the patch at band offset q // 3 - 1 and sector offset q % 3 - 1 (sectors periodic): between 64 and 192 live entries first, then -1. Entry q = 4 and entries towards bands that don't exist hold only -1. Every device fills all 192 slots of its list to one of its two sector neighbours. `far_rows`: entry [p, q] lists own mesh nodes of device p sent to device q: between 5 and 16 live entries first, then -1. A device sends nothing to itself, and every device fills all 16 slots of its list to some other device.
All inputs are finite; a program needn't handle non-finite values.
Results may differ from a plain program's by a relative error of at most 0.006.
Values may be sent and summed in bfloat16 or wider, within the bound.
A program may use at most 128 MiB of HBM per device.

v0:
```python
import jax
import jax.numpy as jnp
from jax import lax
from jax.sharding import PartitionSpec as P

HW = 4


EPS = 1e-05


def with_halo(cells, sides, width):
    for axis, dim in sides:
        count = lax.axis_size(axis)
        head = lax.slice_in_dim(cells, 0, width, axis=dim)
        tail = lax.slice_in_dim(cells, cells.shape[dim] - width, cells.shape[dim], axis=dim)
        cells = jnp.concatenate(
            [
                lax.ppermute(tail, axis, [(i, (i + 1) % count) for i in range(count)]),
                cells,
                lax.ppermute(head, axis, [((i + 1) % count, i) for i in range(count)]),
            ],
            axis=dim,
        )
    return cells


def passed_along(value, axis, steps):
    count = lax.axis_size(axis)
    pairs = [(source, (source + steps) % count) for source in range(count)]
    return lax.ppermute(value, axis, pairs)


def from_behind(block, axis, distance):
    devices = range(lax.axis_size(axis))
    route = [(i - distance, i) for i in devices if i - distance in devices]
    return lax.ppermute(block, axis, route)


def layer_norm(values, norm_pair):
    row_mean = jnp.mean(values, axis=-1, keepdims=True)
    centred = values - row_mean
    variance = jnp.mean(centred * centred, axis=-1, keepdims=True)
    return centred * lax.rsqrt(variance + EPS) * norm_pair[0] + norm_pair[1]


def project(node_rows, weight):
    return jnp.dot(node_rows, weight, preferred_element_type=jnp.float32)


def finish(pre_act, w_out, norm_pair):
    hidden = jax.nn.silu(pre_act).astype(jnp.bfloat16)
    return layer_norm(project(hidden, w_out), norm_pair)


def residual_add(base, branch):
    return (base.astype(jnp.float32) + branch).astype(jnp.bfloat16)


def local_rows(receiver, window):
    return (window[:, None] * 128 + jnp.maximum(receiver, 0)).reshape(-1)


def aggregate(updated, receiver, window, node_count):
    block_count = receiver.shape[0]
    coordinate_spots = jnp.arange(128, dtype=jnp.int32)
    onehot = (receiver[:, :, None] == coordinate_spots[None, None, :]).astype(jnp.bfloat16)
    nodes_per_block = jnp.einsum(
        "zlv,zlo->zvo",
        onehot,
        updated.reshape(block_count, 128, -1),
        preferred_element_type=jnp.float32,
    )
    windows = jnp.arange(node_count // 128, dtype=jnp.int32)
    node_assignment = (window[None, :] == windows[:, None]).astype(jnp.float32)
    message_total = jnp.einsum(
        "za,arf->zrf", node_assignment, nodes_per_block, precision=lax.Precision.HIGHEST
    )
    return message_total.reshape(node_count, -1).astype(jnp.bfloat16)


def body(
    grid_nodes,
    mesh_nodes,
    g2m_edges,
    mesh_edges,
    g2m_sender,
    g2m_receiver,
    g2m_window,
    mesh_sender,
    mesh_receiver,
    mesh_window,
    near_rows,
    far_rows,
    w_g2m_edge,
    w_mesh_node,
    w_grid_node,
    w_proc_edge,
    w_proc_node,
    norms,
):
    latent_width = grid_nodes.shape[-1]
    node_count = mesh_nodes.shape[0]
    haloed = with_halo(grid_nodes, (("lat", 0), ("lon", 1)), HW)
    source_proj = project(haloed.reshape(-1, latent_width), w_g2m_edge[1])
    target_proj = project(mesh_nodes, w_g2m_edge[2])
    g2m_flat = g2m_edges.reshape(-1, latent_width)
    pre_act = (
        project(g2m_flat, w_g2m_edge[0])
        + source_proj[g2m_sender.reshape(-1)]
        + target_proj[local_rows(g2m_receiver, g2m_window)]
    )
    updated = residual_add(g2m_flat, finish(pre_act, w_g2m_edge[3], norms[0]))
    mesh_sum = aggregate(updated, g2m_receiver, g2m_window, node_count)
    node_pre = project(mesh_nodes, w_mesh_node[0]) + project(mesh_sum, w_mesh_node[1])
    mesh_mid = residual_add(mesh_nodes, finish(node_pre, w_mesh_node[2], norms[1]))
    grid_flat = grid_nodes.reshape(-1, latent_width)
    grid_out = residual_add(
        grid_flat, finish(project(grid_flat, w_grid_node[0]), w_grid_node[1], norms[2])
    ).reshape(grid_nodes.shape)
    own_proj = project(mesh_mid, w_proc_edge[1])
    near_lists = near_rows.reshape(9, -1)
    near_slots = near_lists.shape[1]
    near_live = (near_lists >= 0)[:, :, None]
    near_payload = jnp.where(
        near_live, mesh_mid[jnp.maximum(near_lists, 0)], jnp.zeros((), jnp.bfloat16)
    )
    near_payload = near_payload.reshape(3, 3, near_slots, latent_width)
    lon_moved = []
    for offset in (1, -1):
        lon_moved.append(passed_along(near_payload[:, 1 + offset], "lon", offset))
    relayed = jnp.stack([lon_moved[0], near_payload[:, 1], lon_moved[1]], axis=1)
    lat_moved = []
    for offset in (1, -1):
        lat_moved.append(from_behind(relayed[1 + offset], "lat", offset))
    near_arrived = jnp.stack([lat_moved[0], relayed[1], lat_moved[1]], axis=0).reshape(
        -1, latent_width
    )
    near_proj = project(near_arrived, w_proc_edge[1])
    far_lists = far_rows.reshape(-1, far_rows.shape[-1])
    far_live = (far_lists >= 0)[:, :, None]
    picked = jnp.maximum(far_lists, 0)
    payload = jnp.where(far_live, mesh_mid[picked], jnp.zeros((), jnp.bfloat16))
    arrived = lax.all_to_all(payload, ("lat", "lon"), split_axis=0, concat_axis=0, tiled=True)
    far_proj = project(arrived.reshape(-1, latent_width), w_proc_edge[1])
    source_table = jnp.concatenate([own_proj, near_proj, far_proj], axis=0)
    mesh_target = project(mesh_mid, w_proc_edge[2])
    proc_flat = mesh_edges.reshape(-1, latent_width)
    proc_pre = (
        project(proc_flat, w_proc_edge[0])
        + source_table[mesh_sender.reshape(-1)]
        + mesh_target[local_rows(mesh_receiver, mesh_window)]
    )
    proc_updated = residual_add(proc_flat, finish(proc_pre, w_proc_edge[3], norms[3]))
    proc_sum = aggregate(proc_updated, mesh_receiver, mesh_window, node_count)
    out_pre = project(mesh_mid, w_proc_node[0]) + project(proc_sum, w_proc_node[1])
    mesh_out = residual_add(mesh_mid, finish(out_pre, w_proc_node[2], norms[4]))
    return (mesh_out, grid_out)


def solution(mesh):
    return jax.shard_map(
        body,
        mesh=mesh,
        in_specs=(
            P("lat", "lon", None),
            P(("lat", "lon"), None),
            P(("lat", "lon"), None, None),
            P(("lat", "lon"), None, None),
            P(("lat", "lon"), None),
            P(("lat", "lon"), None),
            P(("lat", "lon")),
            P(("lat", "lon"), None),
            P(("lat", "lon"), None),
            P(("lat", "lon")),
            P(("lat", "lon"), None, None),
            P(("lat", "lon"), None, None),
            P(),
            P(),
            P(),
            P(),
            P(),
            P(),
        ),
        out_specs=(P(("lat", "lon"), None), P("lat", "lon", None)),
        check_vma=False,
    )
```

profile of v0, /device:TPU:1, one launch (start us, length us, event | category | flops | bytes accessed | tf_op | source)
XLA Modules:
  0.0 176.2 jit_solution(4387129024968746592)
XLA Ops:
  0.6 1.9 %fusion.97 = (bf16[4,64,512]{2,1,0:T(8,128)(2,1)}, bf16[4,64,512]{2,1,0:T(8,128)(2,1)}) fusion(bf16[16,64,512]{2,1,0:T(8,128)(2,1)} %param.18), kind=kLoop, calls=%fused_computation.145 | loop fusion | bytes 1048576 | tf_op jit(solution)/shard_map/slice | solution.py:15
  2.6 2.7 %collective-permute-start = (bf16[4,64,512]{2,1,0:T(8,128)(2,1)}, bf16[4,64,512]{2,1,0:T(8,128)(2,1)}, u32[]{:S(2)}, u32[]{:S(2)}) collective-permute-start(bf16[4,64,512]{2,1,0:T(8,128)(2,1)} %get-tuple-element.15), channel_id=1, source_target_pairs={{0,16},{16,32},{32,48},{48,64},{64,80},{80,96},{96,112},{112,0},{1... | collective-permute-start | bytes 786440 | tf_op jit(solution)/shard_map/ppermute | solution.py:19
  5.3 0.7 broadcast_maximum_fusion
  6.0 0.7 compare_bitcast_fusion
  6.7 0.7 compare_select_fusion.1
  7.4 0.7 fusion.83
  8.1 0.7 broadcast_multiply_fusion.6
  8.8 1.4 fusion.98
  10.2 1.6 fusion.44
  11.9 2.5 %fusion.54 = f32[512,512]{1,0:T(8,128)} fusion(bf16[512,512]{1,0:T(8,128)(2,1)S(1)} %copy-done.6, bf16[3,512,512]{2,1,0:T(8,128)(2,1)} %param.31), kind=kOutput, calls=%fused_computation.76 | convolution fusion | flops 268435456 | bytes 2097152 | tf_op jit(solution)/shard_map/dot_general | solution.py:48
  14.6 3.0 %fusion.111 = (f32[1024]{0:T(1024)S(1)}, f32[1024,512]{1,0:T(8,128)S(1)}) fusion(bf16[2,512,512]{2,1,0:T(8,128)(2,1)} %param.32, bf16[1024,512]{1,0:T(8,128)(2,1)} %bitcast.173), kind=kOutput, calls=%fused_computation.151 | convolution fusion | flops 1076886528 | bytes 4198400 | tf_op jit(solution)/shard_map/dot_general | solution.py:48
  17.7 0.4 multiply_reduce_fusion.2
  18.1 0.8 add_rsqrt_fusion.2
  18.9 0.6 pad_clamp_fusion.2
  19.6 0.6 broadcast_clamp_fusion.1
  20.3 2.0 %copy.29 = bf16[512,512]{0,1:T(8,128)(2,1)} copy(bf16[512,512]{1,0:T(8,128)(2,1)} %param.19) | data formatting | bytes 1048576 | tf_op args[1]
  22.4 0.6 ge.21
  23.0 0.7 copy.36
  23.7 1.0 constant_dynamic-update-slice_fusion.2
  24.7 1.3 constant_dynamic-update-slice_fusion.1
  26.1 1.1 copy-done.8
  27.3 1.7 collective-permute-start.2
  29.0 4.4 %collective-permute-start.3 = (bf16[24,4,512]{2,1,0:T(4,128)(2,1)S(1)}, bf16[24,4,512]{2,1,0:T(4,128)(2,1)S(1)}, u32[]{:S(2)}, u32[]{:S(2)}) collective-permute-start(bf16[24,4,512]{2,1,0:T(4,128)(2,1)S(1)} %get-tuple-element.13), channel_id=1, source_target_pairs={{1,0},{2,1},{3,2},{4,3},{5,4},{6,5},{7,6},{8,7},{9,8},{10,9},{11,1... | collective-permute-start | bytes 294920 | tf_op jit(solution)/shard_map/ppermute | solution.py:21
  33.4 5.7 %gather_fusion.1 = f32[1792,512]{1,0:T(8,128)} fusion(f32[512,512]{1,0:T(8,128)S(1)} %fusion.44, s32[2048]{0:T(1024)S(1)} %get-tuple-element.37), kind=kCustom, calls=%fused_computation.1 | custom fusion | bytes 7347200 | tf_op jit(solution)/shard_map/gather | solution.py:111
  39.1 1.1 pad_maximum_fusion.1
  40.2 2.1 %fusion.46 = f32[1728,512]{1,0:T(8,128)S(1)} fusion(bf16[1728,512]{1,0:T(8,128)(2,1)S(1)} %bitcast.167, bf16[4,512,512]{2,1,0:T(8,128)(2,1)} %param.30), kind=kOutput, calls=%fused_computation.72 | convolution fusion | flops 905969664 | bytes 5832704 | tf_op jit(solution)/shard_map/dot_general | solution.py:48
  42.3 5.9 %gather_fusion = f32[1792,512]{1,0:T(8,128)} fusion(f32[1728,512]{1,0:T(8,128)S(1)} %fusion.46, s32[2048]{0:T(1024)} %get-tuple-element.38), kind=kCustom, calls=%fused_computation | custom fusion | bytes 7347200 | tf_op jit(solution)/shard_map/gather | solution.py:110
  48.2 8.4 %fusion.99 = (f32[1792]{0:T(1024)S(1)}, f32[1792,512]{1,0:T(8,128)}) fusion(bf16[4,512,512]{2,1,0:T(8,128)(2,1)} %param.30, f32[1792,512]{1,0:T(8,128)} %gather_fusion.1, f32[1792,512]{1,0:T(8,128)} %gather_fusion, bf16[1792,512]{1,0:T(8,128)(2,1)} %bitcast.175), kind=kOutput, calls=%fused_computation.147 | convolution fusion | flops 1886386432 | bytes 13900800 | tf_op jit(solution)/shard_map/dot_general | solution.py:48
  56.6 2.8 %multiply_reduce_fusion.1 = f32[1792]{0:T(1024)S(1)} fusion(f32[1792,512]{1,0:T(8,128)} %get-tuple-element.27, f32[1792]{0:T(1024)S(1)} %broadcast_multiply_fusion.1), kind=kLoop, calls=%fused_computation.15 | loop fusion | flops 2750720 | bytes 3684352 | tf_op jit(solution)/shard_map/reduce_sum | solution.py:43
  59.7 1.2 add_convert_fusion.1
  60.9 1.6 fusion.16
  62.6 3.7 %fusion.6 = bf16[4,128,512]{2,0,1:T(4,128)(2,1)S(1)} fusion(f32[14,128,512]{2,1,0:T(8,128)S(1)} %fusion.16, s32[14]{0:T(128)S(1)} %copy-done.38), kind=kOutput, calls=%fused_computation.29 | convolution fusion | flops 44302392 | bytes 4194360 | tf_op jit(solution)/shard_map/za,arf->zrf/dot_general | solution.py:76
  66.4 2.3 %fusion.102 = (f32[512]{0:T(512)S(1)}, f32[512,512]{0,1:T(8,128)S(1)}) fusion(bf16[3,512,512]{2,1,0:T(8,128)(2,1)} %param.31, f32[512,512]{1,0:T(8,128)S(1)} %copy-done.14, bf16[512,512]{1,0:T(8,128)(2,1)S(1)} %bitcast.178), kind=kOutput, calls=%fused_computation.148 | convolution fusion | flops 538705408 | bytes 3672064 | tf_op jit(solution)/shard_map/dot_general | solution.py:48
  69.4 5.7 %gather_fusion.2 = bf16[1728,512]{1,0:T(8,128)(2,1)S(1)} fusion(bf16[512,512]{1,0:T(8,128)(2,1)S(1)} %copy.31, s32[2048]{0:T(1024)S(1)} %get-tuple-element.36), kind=kCustom, calls=%fused_computation.2 | custom fusion | bytes 3545856 | tf_op jit(solution)/shard_map/gather | solution.py:126
  75.2 0.3 broadcast_select_fusion.1
  75.5 1.2 slice_bitcast_fusion.5
  76.7 4.8 %collective-permute-start.5 = (bf16[3,192,512]{2,1,0:T(8,128)(2,1)}, bf16[3,192,512]{2,1,0:T(8,128)(2,1)}, u32[]{:S(2)}, u32[]{:S(2)}) collective-permute-start(bf16[3,192,512]{2,1,0:T(8,128)(2,1)} %get-tuple-element.10), channel_id=1, source_target_pairs={{0,15},{1,0},{2,1},{3,2},{4,3},{5,4},{6,5},{7,6},{8,7},{9,8},{10,9... | collective-permute-start | bytes 1769480 | tf_op jit(solution)/shard_map/ppermute | solution.py:31
  81.5 7.5 %gather_fusion.3 = bf16[2048,512]{1,0:T(8,128)(2,1)S(1)} fusion(bf16[512,512]{1,0:T(8,128)(2,1)S(1)} %copy.31, s32[2048]{0:T(1024)S(1)} %get-tuple-element.41), kind=kCustom, calls=%fused_computation.3 | custom fusion | bytes 4202496 | tf_op jit(solution)/shard_map/gather | solution.py:143
  89.1 1.5 broadcast_select_fusion
  90.6 7.3 %all-to-all-start = ((bf16[128,16,512]{2,1,0:T(8,128)(2,1)}), bf16[128,16,512]{2,1,0:T(8,128)(2,1)}, u32[]{:S(2)}, u32[]{:S(2)}) async-start(bf16[128,16,512]{2,1,0:T(8,128)(2,1)} %broadcast_select_fusion), calls=%async_computation | async-start | bytes 4194304 | tf_op jit(solution)/shard_map/all_to_all | solution.py:144
  98.0 2.8 %add_convert_fusion.2 = bf16[1024,512]{1,0:T(8,128)(2,1)} fusion(f32[1024,512]{1,0:T(8,128)S(1)} %copy-done.5, f32[512]{0:T(512)S(1)} %bitcast.184, f32[512]{0:T(512)S(1)} %bitcast.183, f32[1024]{0:T(1024)S(1)} %copy-done.26, f32[1024]{0:T(1024)S(1)} %copy-done.18, bf16[16,64,512]{2,1,0:T(8,128)(2,1)} %param.18), kind=kLoop, calls=%fused_computation.17 | loop fusion | flops 3670016 | bytes 4206592 | tf_op jit(solution)/shard_map/convert_element_type | solution.py:57
  100.7 1.4 pad_maximum_fusion.2
  102.2 1.0 slice_bitcast_fusion.2
  103.2 3.6 %collective-permute-start.6 = (bf16[3,192,512]{2,1,0:T(8,128)(2,1)}, bf16[3,192,512]{2,1,0:T(8,128)(2,1)S(1)}, u32[]{:S(2)}, u32[]{:S(2)}) collective-permute-start(bf16[3,192,512]{2,1,0:T(8,128)(2,1)} %get-tuple-element.6), channel_id=1, source_target_pairs={{0,16},{16,32},{32,48},{48,64},{64,80},{80,96},{96,112},{1,17},{17... | collective-permute-start | bytes 1769480 | tf_op jit(solution)/shard_map/ppermute | solution.py:37
  106.8 1.9 %collective-permute-start.7 = (bf16[3,192,512]{2,1,0:T(8,128)(2,1)S(1)}, bf16[3,192,512]{2,1,0:T(8,128)(2,1)}, u32[]{:S(2)}, u32[]{:S(2)}) collective-permute-start(bf16[3,192,512]{2,1,0:T(8,128)(2,1)S(1)} %get-tuple-element.7), channel_id=1, source_target_pairs={{16,0},{32,16},{48,32},{64,48},{80,64},{96,80},{112,96},{17,1},{33... | collective-permute-start | bytes 1769480 | tf_op jit(solution)/shard_map/ppermute | solution.py:37
  108.7 1.5 fusion.28
  110.2 9.2 %gather_fusion.5 = f32[2048,512]{1,0:T(8,128)} fusion(f32[512,512]{1,0:T(8,128)S(1)} %fusion.28, s32[2048]{0:T(1024)S(1)} %copy-done.25), kind=kCustom, calls=%fused_computation.5 | custom fusion | bytes 8396800 | tf_op jit(solution)/shard_map/gather | solution.py:152
  119.4 2.5 %fusion.34 = f32[512,512]{1,0:T(8,128)} fusion(bf16[512,512]{0,1:T(8,128)(2,1)S(1)} %add_convert_fusion.4, bf16[4,512,512]{2,1,0:T(8,128)(2,1)} %param.33), kind=kOutput, calls=%fused_computation.62 | convolution fusion | flops 268435456 | bytes 2097152 | tf_op jit(solution)/shard_map/dot_general | solution.py:48
  121.9 2.5 %fusion.38 = f32[512,512]{1,0:T(8,128)} fusion(bf16[512,512]{0,1:T(8,128)(2,1)S(1)} %add_convert_fusion.4, bf16[3,512,512]{2,1,0:T(8,128)(2,1)} %param.34), kind=kOutput, calls=%fused_computation.65 | convolution fusion | flops 268435456 | bytes 2097152 | tf_op jit(solution)/shard_map/dot_general | solution.py:48
  124.4 1.8 collective-permute-done.6
  126.2 1.9 %collective-permute-done.7 = bf16[3,192,512]{2,1,0:T(8,128)(2,1)} collective-permute-done((bf16[3,192,512]{2,1,0:T(8,128)(2,1)S(1)}, bf16[3,192,512]{2,1,0:T(8,128)(2,1)}, u32[]{:S(2)}, u32[]{:S(2)}) %collective-permute-start.7) | collective-permute-done | bytes 589856 | tf_op jit(solution)/shard_map/ppermute | solution.py:37
  128.1 1.3 pad_maximum_fusion.3
  129.3 2.1 %fusion.32 = f32[1728,512]{1,0:T(8,128)S(1)} fusion(bf16[1728,512]{1,0:T(8,128)(2,1)S(1)} %bitcast.168, bf16[4,512,512]{2,1,0:T(8,128)(2,1)} %param.33), kind=kOutput, calls=%fused_computation.60 | convolution fusion | flops 905969664 | bytes 5832704 | tf_op jit(solution)/shard_map/dot_general | solution.py:48
  131.5 3.0 %fusion.30 = f32[2048,512]{1,0:T(8,128)S(1)} fusion(bf16[2048,512]{1,0:T(8,128)(2,1)} %bitcast.33, bf16[4,512,512]{2,1,0:T(8,128)(2,1)} %param.33), kind=kOutput, calls=%fused_computation.58 | convolution fusion | flops 1073741824 | bytes 6815744 | tf_op jit(solution)/shard_map/dot_general | solution.py:48
  134.5 4.1 %pad_maximum_fusion = f32[4288,512]{1,0:T(8,128)} fusion(f32[2048,512]{1,0:T(8,128)S(1)} %fusion.30, f32[1728,512]{1,0:T(8,128)S(1)} %fusion.32, f32[512,512]{1,0:T(8,128)S(1)} %copy-done.7), kind=kLoop, calls=%fused_computation.6 | loop fusion | flops 4390912 | bytes 17563648 | tf_op jit(solution)/shard_map/concatenate | solution.py:146
  138.6 13.2 %gather_fusion.4 = f32[2048,512]{1,0:T(8,128)} fusion(f32[4288,512]{1,0:T(8,128)} %pad_maximum_fusion, s32[2048]{0:T(1024)S(1)} %copy-done.24), kind=kCustom, calls=%fused_computation.4 | custom fusion | bytes 8396800 | tf_op jit(solution)/shard_map/gather | solution.py:151
  151.8 8.7 %fusion.105 = (f32[2048]{0:T(1024)S(1)}, f32[2048,512]{1,0:T(8,128)}) fusion(bf16[4,512,512]{2,1,0:T(8,128)(2,1)S(1)} %copy-done.11, f32[2048,512]{1,0:T(8,128)} %gather_fusion.5, f32[2048,512]{1,0:T(8,128)} %gather_fusion.4, bf16[2048,512]{1,0:T(8,128)(2,1)} %bitcast.174), kind=kOutput, calls=%fused_computation.149 | convolution fusion | flops 2155870208 | bytes 15736832 | tf_op jit(solution)/shard_map/dot_general | solution.py:48
  160.5 3.0 %multiply_reduce_fusion = f32[2048]{0:T(1024)S(1)} fusion(f32[2048,512]{1,0:T(8,128)} %get-tuple-element.31, f32[2048]{0:T(1024)S(1)} %broadcast_multiply_fusion), kind=kLoop, calls=%fused_computation.12 | loop fusion | flops 3143680 | bytes 4210688 | tf_op jit(solution)/shard_map/reduce_sum | solution.py:43
  163.6 0.4 copy-done.2
  164.0 2.3 %add_convert_fusion = bf16[2048,512]{1,0:T(8,128)(2,1)S(1)} fusion(f32[2048,512]{1,0:T(8,128)S(1)} %copy-done.2, f32[512]{0:T(512)S(1)} %bitcast.193, f32[512]{0:T(512)S(1)} %bitcast.194, f32[2048]{0:T(1024)S(1)} %add_rsqrt_fusion, f32[2048]{0:T(1024)S(1)} %broadcast_multiply_fusion, bf16[16,128,512]{2,1,0:T(8,128)(2,1)} %param.21), kind=kLoop, calls=%fused_computation.11 | loop fusion | flops 7340032 | bytes 8409088 | tf_op jit(solution)/shard_map/convert_element_type | solution.py:57
  166.3 1.9 %fusion.15 = f32[16,128,512]{2,1,0:T(8,128)S(1)} fusion(bf16[16,128,512]{2,1,0:T(8,128)(2,1)S(1)} %bitcast.170, s32[16,128]{1,0:T(8,128)S(1)} %copy-done.23), kind=kOutput, calls=%fused_computation.41 | convolution fusion | flops 268697600 | bytes 6299648 | tf_op jit(solution)/shard_map/zlv,zlo->zvo/dot_general | solution.py:68
  168.3 3.9 %fusion.9 = bf16[4,128,512]{2,0,1:T(4,128)(2,1)S(1)} fusion(f32[16,128,512]{2,1,0:T(8,128)S(1)} %fusion.15, s32[16]{0:T(128)S(1)} %copy-done.40), kind=kOutput, calls=%fused_computation.30 | convolution fusion | flops 50593856 | bytes 4718656 | tf_op jit(solution)/shard_map/za,arf->zrf/dot_general | solution.py:76
  172.4 2.3 %fusion.108 = (f32[512]{0:T(512)S(1)}, f32[512,512]{0,1:T(8,128)S(1)}) fusion(bf16[3,512,512]{2,1,0:T(8,128)(2,1)} %param.34, f32[512,512]{1,0:T(8,128)S(1)} %copy-done.15, bf16[512,512]{1,0:T(8,128)(2,1)S(1)} %bitcast.179), kind=kOutput, calls=%fused_computation.150 | convolution fusion | flops 538705408 | bytes 3672064 | tf_op jit(solution)/shard_map/dot_general | solution.py:48
  175.2 1.0 copy.40
  (118 shorter events, 2.5 us)
Async XLA Ops:
  0.6 11.2 %copy-start.6 = (bf16[512,512]{1,0:T(8,128)(2,1)S(1)}, bf16[512,512]{1,0:T(8,128)(2,1)}, u32[]{:S(2)}) copy-start(bf16[512,512]{1,0:T(8,128)(2,1)} %param.19) | copy-start | bytes 1572868
  2.6 21.2 %collective-permute-start = (bf16[4,64,512]{2,1,0:T(8,128)(2,1)}, bf16[4,64,512]{2,1,0:T(8,128)(2,1)}, u32[]{:S(2)}, u32[]{:S(2)}) collective-permute-start(bf16[4,64,512]{2,1,0:T(8,128)(2,1)} %get-tuple-element.15), channel_id=1, source_target_pairs={{0,16},{16,32},{32,48},{48,64},{64,80},{80,96},{96,112},{112,0},{1... | collective-permute-start | bytes 786440 | tf_op jit(solution)/shard_map/ppermute | solution.py:19
  5.3 20.8 %collective-permute-start.1 = (bf16[4,64,512]{2,1,0:T(8,128)(2,1)}, bf16[4,64,512]{2,1,0:T(8,128)(2,1)S(1)}, u32[]{:S(2)}, u32[]{:S(2)}) collective-permute-start(bf16[4,64,512]{2,1,0:T(8,128)(2,1)} %get-tuple-element.14), channel_id=1, source_target_pairs={{16,0},{32,16},{48,32},{64,48},{80,64},{96,80},{112,96},{0,112},{1... | collective-permute-start | bytes 786440 | tf_op jit(solution)/shard_map/ppermute | solution.py:21
  10.2 4.3 %copy-start.39 = (s32[16]{0:T(128)S(1)}, s32[16]{0:T(128)}, u32[]{:S(2)}) copy-start(s32[16]{0:T(128)} %param.27) | copy-start | bytes 196
  10.2 4.3 %copy-start.22 = (s32[16,128]{1,0:T(8,128)S(1)}, s32[16,128]{1,0:T(8,128)}, u32[]{:S(2)}) copy-start(s32[16,128]{1,0:T(8,128)} %param.26) | copy-start | bytes 24580
  17.6 8.4 %copy-start.4 = (f32[1024,512]{1,0:T(8,128)}, f32[1024,512]{1,0:T(8,128)S(1)}, u32[]{:S(2)}) copy-start(f32[1024,512]{1,0:T(8,128)S(1)} %get-tuple-element.35) | copy-start | bytes 6291460
  17.6 1.9 %copy-start.20 = (s32[14,128]{1,0:T(8,128)S(1)}, s32[14,128]{1,0:T(8,128)}, u32[]{:S(2)}) copy-start(s32[14,128]{1,0:T(8,128)} %param.23) | copy-start | bytes 21508
  17.6 2.5 %copy-start.19 = (s32[1,9,192]{2,0,1:T(1,128)S(1)}, s32[1,9,192]{2,0,1:T(1,128)}, u32[]{:S(2)}) copy-start(s32[1,9,192]{2,0,1:T(1,128)} %param.28) | copy-start | bytes 20740
  17.7 1.9 %copy-start.17 = (f32[1024]{0:T(1024)}, f32[1024]{0:T(1024)S(1)}, u32[]{:S(2)}) copy-start(f32[1024]{0:T(1024)S(1)} %broadcast_multiply_fusion.2) | copy-start | bytes 12292
  26.1 1.2 copy-start.8
  27.3 11.8 %collective-permute-start.2 = (bf16[24,4,512]{2,1,0:T(4,128)(2,1)S(1)}, bf16[24,4,512]{2,1,0:T(4,128)(2,1)S(1)}, u32[]{:S(2)}, u32[]{:S(2)}) collective-permute-start(bf16[24,4,512]{2,1,0:T(4,128)(2,1)S(1)} %get-tuple-element.12), channel_id=1, source_target_pairs={{0,1},{1,2},{2,3},{3,4},{4,5},{5,6},{6,7},{7,8},{8,9},{9,10},{10,1... | collective-permute-start | bytes 294920 | tf_op jit(solution)/shard_map/ppermute | solution.py:19
  29.0 10.1 %collective-permute-start.3 = (bf16[24,4,512]{2,1,0:T(4,128)(2,1)S(1)}, bf16[24,4,512]{2,1,0:T(4,128)(2,1)S(1)}, u32[]{:S(2)}, u32[]{:S(2)}) collective-permute-start(bf16[24,4,512]{2,1,0:T(4,128)(2,1)S(1)} %get-tuple-element.13), channel_id=1, source_target_pairs={{1,0},{2,1},{3,2},{4,3},{5,4},{6,5},{7,6},{8,7},{9,8},{10,9},{11,1... | collective-permute-start | bytes 294920 | tf_op jit(solution)/shard_map/ppermute | solution.py:21
  33.4 5.7 %copy-start.9 = (bf16[24,64,512]{2,1,0:T(8,128)(2,1)S(1)}, bf16[24,64,512]{2,1,0:T(8,128)(2,1)}, u32[]{:S(2)}) copy-start(bf16[24,64,512]{2,1,0:T(8,128)(2,1)} %copy-done.8) | copy-start | bytes 4718596
  48.2 11.2 %copy-start.13 = (bf16[14,128,512]{2,1,0:T(8,128)(2,1)S(1)}, bf16[14,128,512]{2,1,0:T(8,128)(2,1)}, u32[]{:S(2)}) copy-start(bf16[14,128,512]{2,1,0:T(8,128)(2,1)} %param.20) | copy-start | bytes 5505028
  56.5 3.1 %copy-start.3 = (f32[1792,512]{1,0:T(8,128)S(1)}, f32[1792,512]{1,0:T(8,128)}, u32[]{:S(2)}) copy-start(f32[1792,512]{1,0:T(8,128)} %get-tuple-element.27) | copy-start | bytes 11010052
  56.5 3.1 %copy-start.30 = (f32[1,1,512]{2,1,0:T(1,128)S(1)}, f32[1,1,512]{2,1,0:T(1,128)}, u32[]{:S(2)}) copy-start(f32[1,1,512]{2,1,0:T(1,128)} %get-tuple-element.23) | copy-start | bytes 6148
  56.5 3.1 %copy-start.31 = (f32[1,1,512]{2,1,0:T(1,128)S(1)}, f32[1,1,512]{2,1,0:T(1,128)}, u32[]{:S(2)}) copy-start(f32[1,1,512]{2,1,0:T(1,128)} %get-tuple-element.24) | copy-start | bytes 6148
  59.7 1.2 copy-start.21
  60.9 1.6 copy-start.38
  62.6 3.8 %copy-start.14 = (f32[512,512]{1,0:T(8,128)S(1)}, f32[512,512]{1,0:T(8,128)}, u32[]{:S(2)}) copy-start(f32[512,512]{1,0:T(8,128)} %fusion.54) | copy-start | bytes 3145732
  66.4 2.5 %copy-start.12 = (bf16[512,512]{0,1:T(8,128)(2,1)S(1)}, bf16[512,512]{0,1:T(8,128)(2,1)}, u32[]{:S(2)}) copy-start(bf16[512,512]{0,1:T(8,128)(2,1)} %copy.29) | copy-start | bytes 1572868
  66.4 2.5 %copy-start.34 = (f32[1,1,512]{2,1,0:T(1,128)S(1)}, f32[1,1,512]{2,1,0:T(1,128)}, u32[]{:S(2)}) copy-start(f32[1,1,512]{2,1,0:T(1,128)} %get-tuple-element.21) | copy-start | bytes 6148
  66.4 2.5 %copy-start.35 = (f32[1,1,512]{2,1,0:T(1,128)S(1)}, f32[1,1,512]{2,1,0:T(1,128)}, u32[]{:S(2)}) copy-start(f32[1,1,512]{2,1,0:T(1,128)} %get-tuple-element.22) | copy-start | bytes 6148
  69.2 52.7 %copy-start = (bf16[512,512]{0,1:T(8,128)(2,1)}, bf16[512,512]{0,1:T(8,128)(2,1)S(1)}, u32[]{:S(2)}) copy-start(bf16[512,512]{0,1:T(8,128)(2,1)S(1)} %add_convert_fusion.4) | copy-start | bytes 1572868
  69.4 5.7 %copy-start.27 = (pred[3,3,192]{2,1,0:T(4,128)(4,1)S(1)}, pred[3,3,192]{2,1,0:T(4,128)(4,1)}, u32[]{:S(2)}) copy-start(pred[3,3,192]{2,1,0:T(4,128)(4,1)} %ge.21) | copy-start | bytes 5188
  76.7 24.0 %collective-permute-start.4 = (bf16[3,192,512]{2,1,0:T(8,128)(2,1)}, bf16[3,192,512]{2,1,0:T(8,128)(2,1)}, u32[]{:S(2)}, u32[]{:S(2)}) collective-permute-start(bf16[3,192,512]{2,1,0:T(8,128)(2,1)} %get-tuple-element.9), channel_id=1, source_target_pairs={{0,1},{1,2},{2,3},{3,4},{4,5},{5,6},{6,7},{7,8},{8,9},{9,10},{10,1... | collective-permute-start | bytes 1769480 | tf_op jit(solution)/shard_map/ppermute | solution.py:31
  76.7 24.0 %collective-permute-start.5 = (bf16[3,192,512]{2,1,0:T(8,128)(2,1)}, bf16[3,192,512]{2,1,0:T(8,128)(2,1)}, u32[]{:S(2)}, u32[]{:S(2)}) collective-permute-start(bf16[3,192,512]{2,1,0:T(8,128)(2,1)} %get-tuple-element.10), channel_id=1, source_target_pairs={{0,15},{1,0},{2,1},{3,2},{4,3},{5,4},{6,5},{7,6},{8,7},{9,8},{10,9... | collective-permute-start | bytes 1769480 | tf_op jit(solution)/shard_map/ppermute | solution.py:31
  81.5 7.5 %copy-start.16 = (pred[128,16]{1,0:T(8,128)(4,1)S(1)}, pred[128,16]{1,0:T(8,128)(4,1)}, u32[]{:S(2)}) copy-start(pred[128,16]{1,0:T(8,128)(4,1)} %copy.36) | copy-start | bytes 6148
  90.6 7.3 %copy-start.5 = (f32[1024,512]{1,0:T(8,128)S(1)}, f32[1024,512]{1,0:T(8,128)}, u32[]{:S(2)}) copy-start(f32[1024,512]{1,0:T(8,128)} %copy-done.4) | copy-start | bytes 6291460
  90.6 7.3 %copy-start.18 = (f32[1024]{0:T(1024)S(1)}, f32[1024]{0:T(1024)}, u32[]{:S(2)}) copy-start(f32[1024]{0:T(1024)} %copy-done.17) | copy-start | bytes 12292
  90.6 7.3 %copy-start.26 = (f32[1024]{0:T(1024)S(1)}, f32[1024]{0:T(1024)}, u32[]{:S(2)}) copy-start(f32[1024]{0:T(1024)} %add_rsqrt_fusion.2) | copy-start | bytes 12292
  90.6 7.3 %copy-start.28 = (f32[1,1,512]{2,1,0:T(1,128)S(1)}, f32[1,1,512]{2,1,0:T(1,128)}, u32[]{:S(2)}) copy-start(f32[1,1,512]{2,1,0:T(1,128)} %get-tuple-element.16) | copy-start | bytes 6148
  90.6 7.3 %copy-start.29 = (f32[1,1,512]{2,1,0:T(1,128)S(1)}, f32[1,1,512]{2,1,0:T(1,128)}, u32[]{:S(2)}) copy-start(f32[1,1,512]{2,1,0:T(1,128)} %get-tuple-element.25) | copy-start | bytes 6148
  90.6 40.8 %all-to-all-start = ((bf16[128,16,512]{2,1,0:T(8,128)(2,1)}), bf16[128,16,512]{2,1,0:T(8,128)(2,1)}, u32[]{:S(2)}, u32[]{:S(2)}) async-start(bf16[128,16,512]{2,1,0:T(8,128)(2,1)} %broadcast_select_fusion), calls=%async_computation | async-start | bytes 4194304 | tf_op jit(solution)/shard_map/all_to_all | solution.py:144
  97.9 2.8 %copy-start.10 = (bf16[3,1,192,512]{3,2,0,1:T(8,128)(2,1)S(1)}, bf16[3,1,192,512]{3,2,0,1:T(8,128)(2,1)}, u32[]{:S(2)}) copy-start(bf16[3,1,192,512]{3,2,0,1:T(8,128)(2,1)} %get-tuple-element.11) | copy-start | bytes 1769476
  102.2 8.0 %copy-start.25 = (s32[2048]{0:T(1024)S(1)}, s32[2048]{0:T(1024)}, u32[]{:S(2)}) copy-start(s32[2048]{0:T(1024)} %get-tuple-element.40) | copy-start | bytes 24580
  103.2 23.0 %collective-permute-start.6 = (bf16[3,192,512]{2,1,0:T(8,128)(2,1)}, bf16[3,192,512]{2,1,0:T(8,128)(2,1)S(1)}, u32[]{:S(2)}, u32[]{:S(2)}) collective-permute-start(bf16[3,192,512]{2,1,0:T(8,128)(2,1)} %get-tuple-element.6), channel_id=1, source_target_pairs={{0,16},{16,32},{32,48},{48,64},{64,80},{80,96},{96,112},{1,17},{17... | collective-permute-start | bytes 1769480 | tf_op jit(solution)/shard_map/ppermute | solution.py:37
  106.8 21.3 %collective-permute-start.7 = (bf16[3,192,512]{2,1,0:T(8,128)(2,1)S(1)}, bf16[3,192,512]{2,1,0:T(8,128)(2,1)}, u32[]{:S(2)}, u32[]{:S(2)}) collective-permute-start(bf16[3,192,512]{2,1,0:T(8,128)(2,1)S(1)} %get-tuple-element.7), channel_id=1, source_target_pairs={{16,0},{32,16},{48,32},{64,48},{80,64},{96,80},{112,96},{17,1},{33... | collective-permute-start | bytes 1769480 | tf_op jit(solution)/shard_map/ppermute | solution.py:37
  131.5 3.0 %copy-start.7 = (f32[512,512]{1,0:T(8,128)S(1)}, f32[512,512]{1,0:T(8,128)}, u32[]{:S(2)}) copy-start(f32[512,512]{1,0:T(8,128)} %fusion.34) | copy-start | bytes 3145732
  134.5 4.1 %copy-start.24 = (s32[2048]{0:T(1024)S(1)}, s32[2048]{0:T(1024)}, u32[]{:S(2)}) copy-start(s32[2048]{0:T(1024)} %get-tuple-element.39) | copy-start | bytes 24580
  138.6 13.2 %copy-start.11 = (bf16[4,512,512]{2,1,0:T(8,128)(2,1)S(1)}, bf16[4,512,512]{2,1,0:T(8,128)(2,1)}, u32[]{:S(2)}) copy-start(bf16[4,512,512]{2,1,0:T(8,128)(2,1)} %param.33) | copy-start | bytes 6291460
  160.5 3.4 %copy-start.2 = (f32[2048,512]{1,0:T(8,128)S(1)}, f32[2048,512]{1,0:T(8,128)}, u32[]{:S(2)}) copy-start(f32[2048,512]{1,0:T(8,128)} %get-tuple-element.31) | copy-start | bytes 12582916
  160.5 3.4 %copy-start.36 = (f32[1,1,512]{2,1,0:T(1,128)S(1)}, f32[1,1,512]{2,1,0:T(1,128)}, u32[]{:S(2)}) copy-start(f32[1,1,512]{2,1,0:T(1,128)} %get-tuple-element.19) | copy-start | bytes 6148
  160.5 3.5 %copy-start.37 = (f32[1,1,512]{2,1,0:T(1,128)S(1)}, f32[1,1,512]{2,1,0:T(1,128)}, u32[]{:S(2)}) copy-start(f32[1,1,512]{2,1,0:T(1,128)} %get-tuple-element.20) | copy-start | bytes 6148
  164.0 2.4 %copy-start.23 = (s32[16,128]{1,0:T(8,128)S(1)}, s32[16,128]{1,0:T(8,128)}, u32[]{:S(2)}) copy-start(s32[16,128]{1,0:T(8,128)} %param.26) | copy-start | bytes 24580
  166.3 2.0 %copy-start.40 = (s32[16]{0:T(128)S(1)}, s32[16]{0:T(128)}, u32[]{:S(2)}) copy-start(s32[16]{0:T(128)} %param.27) | copy-start | bytes 196
  168.3 4.0 %copy-start.15 = (f32[512,512]{1,0:T(8,128)S(1)}, f32[512,512]{1,0:T(8,128)}, u32[]{:S(2)}) copy-start(f32[512,512]{1,0:T(8,128)} %fusion.38) | copy-start | bytes 3145732
  172.3 2.5 %copy-start.1 = (bf16[512,512]{0,1:T(8,128)(2,1)S(1)}, bf16[512,512]{0,1:T(8,128)(2,1)}, u32[]{:S(2)}) copy-start(bf16[512,512]{0,1:T(8,128)(2,1)} %copy-done) | copy-start | bytes 1572868
  172.4 2.5 %copy-start.32 = (f32[1,1,512]{2,1,0:T(1,128)S(1)}, f32[1,1,512]{2,1,0:T(1,128)}, u32[]{:S(2)}) copy-start(f32[1,1,512]{2,1,0:T(1,128)} %get-tuple-element.17) | copy-start | bytes 6148
  172.4 2.5 %copy-start.33 = (f32[1,1,512]{2,1,0:T(1,128)S(1)}, f32[1,1,512]{2,1,0:T(1,128)}, u32[]{:S(2)}) copy-start(f32[1,1,512]{2,1,0:T(1,128)} %get-tuple-element.18) | copy-start | bytes 6148
where the time goes:
time: 177 us; the launch traced here: 176 us
  local copies, waits for them, and re-layouts  62.2 us (35%)
  matrix products  53.6 us (30%)
  other arithmetic  29 us (16%)
  starting transfers between devices  26.3 us (15%)
  waiting for transfers between devices  3.66 us (2%)
    dot_general x13, matrix products, project(): return jnp.dot(node_rows, weight, preferred_element_type=jnp.float32)  42.5 us
    gather x1, local copies, waits for them, and re-layouts, body(): source_table[mesh_sender.reshape(-1)]  13.2 us
    gather x1, local copies, waits for them, and re-layouts, body(): mesh_target[local_rows(mesh_receiver, mesh_window)]  9.19 us
    dot_general x2, matrix products, aggregate(): jnp.einsum('za,arf->zrf', node_assignment, nodes_per_block, precision=lax...  7.58 us
    gather x1, local copies, waits for them, and re-layouts, body(): payload = jnp.where(far_live, mesh_mid[picked], jnp.zeros((), jnp.bfloat16))  7.53 us
    unnamed x86, local copies, waits for them, and re-layouts  7.32 us
    all_to_all x1, starting transfers between devices, body(): lax.all_to_all(payload, ('lat', 'lon'), split_axis=0, concat_axis=0, tile...  7.25 us
    convert_element_type x5, other arithmetic, residual_add(): return (base.astype(jnp.float32) + branch).astype(jnp.bfloat16)  6.89 us
  transfers between devices with their start and end apart: 9, of which 2 were waited for; matrix products, arithmetic and copies ran while one was open for 34% of the time, Pallas kernels for 0%

commit v1 on v0

v1 whole, which is shorter than its diff:
```python
import jax
import jax.numpy as jnp
from jax import lax
from jax.experimental import pallas as pl
from jax.experimental.pallas import tpu as pltpu
from jax.sharding import PartitionSpec as P

HW = 4
EPS = 1e-05
D = 512
BF16 = jnp.bfloat16
F32 = jnp.float32
MESH = pl.DeviceIdType.MESH

GRID = 1024
HALO = 704
HALO_PAD = 768
NODES = 512
NCAP = 192
NEAR = 9 * NCAP
NEAR_PAD = 1792
FAR = 16
DEVICES = 128
G_EDGES = 1792
P_EDGES = 2048
STEP = 256

G_POS, G_ROW, P_POS, P_ROW, NEAR_IDX, FAR_IDX = 0, 14, 28, 44, 60, 74

FAR_MUL = 77
FAR_INV = 5
FAR_GROUPS = 4
ROUNDS = 7

SEGMENTS = (
    (1, 0, 0, 256),
    (-1, 0, 256, 256),
    (0, 1, 512, 64),
    (0, -1, 576, 64),
    (1, 1, 640, 16),
    (1, -1, 656, 16),
    (-1, 1, 672, 16),
    (-1, -1, 688, 16),
)


def dot(a, b):
    return jnp.dot(a, b, preferred_element_type=F32)


def silu(v):
    half = 0.5 * v
    return (half + half * jnp.tanh(half)).astype(BF16)


def layer_norm(values, gain, shift):
    mean = jnp.mean(values, axis=-1, keepdims=True)
    centred = values - mean
    variance = jnp.mean(centred * centred, axis=-1, keepdims=True)
    return centred * lax.rsqrt(variance + EPS) * gain + shift


def kernel(
    idx, norms,
    grid_h, mesh_h, ge_h, pe_h, wg_h, wm_h, wr_h, wp_h, wn_h,
    mesh_out, grid_out,
    grid, halo, strips, mesh, ge, pe, wg, wm, wr, wp, wn,
    pre, src, total, node_pre, mid, near_out, near_in, far_out, far_in, gout, mout,
    load_sem, store_sem, halo_send, halo_recv, near_send, near_recv, far_send, far_recv, rounds,
):
    lat, lon = lax.axis_index("lat"), lax.axis_index("lon")
    me = lat * 16 + lon

    def device(p):
        return (lax.div(p, 16), lax.rem(p, 16))

    def neighbour(band, sector):
        return (lax.rem(lat + band + 8, 8), lax.rem(lon + sector + 16, 16))

    loads = [
        pltpu.make_async_copy(h, v, load_sem.at[i])
        for i, (h, v) in enumerate(
            ((grid_h, grid), (ge_h, ge), (mesh_h, mesh), (wg_h, wg), (wm_h, wm),
             (wp_h, wp), (pe_h, pe), (wr_h, wr), (wn_h, wn))
        )
    ]
    for copy in loads:
        copy.start()
    l_grid, l_ge, l_mesh, l_wg, l_wm, l_wp, l_pe, l_wr, l_wn = loads

    halo[pl.ds(HALO, HALO_PAD - HALO), :] = jnp.zeros((HALO_PAD - HALO, D), BF16)
    near_in[pl.ds(4 * NCAP, NCAP), :] = jnp.zeros((NCAP, D), BF16)
    near_in[pl.ds(NEAR, NEAR_PAD - NEAR), :] = jnp.zeros((NEAR_PAD - NEAR, D), BF16)
    far_in[pl.ds(0, FAR), :] = jnp.zeros((FAR, D), BF16)

    barrier = pltpu.get_barrier_semaphore()
    for band, sector, _, _ in SEGMENTS:
        pl.semaphore_signal(barrier, inc=1, device_id=neighbour(band, sector), device_id_type=MESH)
    for r in range(ROUNDS):
        pl.semaphore_signal(
            barrier, inc=1, device_id=device(lax.rem(me + DEVICES - 2**r, DEVICES)), device_id_type=MESH
        )

    def round_start(r):
        pl.semaphore_signal(
            rounds.at[r], inc=1, device_id=device(lax.rem(me + 2**r, DEVICES)), device_id_type=MESH
        )

    def round_end(r):
        pl.semaphore_wait(rounds.at[r], 1)

    lane = lax.broadcasted_iota(jnp.int32, (128, 128), 1)

    def offsets(first, b):
        row = idx[pl.ds(first + b, 1), :]
        return jnp.broadcast_to(row, (128, 128)).T - lane

    def pair(first, step):
        return jnp.concatenate([offsets(first, 2 * step), offsets(first, 2 * step + 1)], axis=0)

    def onehot(off, base, count):
        return jnp.concatenate(
            [jnp.where(off == base + 128 * k, 1.0, 0.0).astype(BF16) for k in range(count // 128)],
            axis=1,
        )

    def onehot_rows(first, step):
        row = jnp.concatenate(
            [idx[pl.ds(first + 2 * step, 1), :], idx[pl.ds(first + 2 * step + 1, 1), :]], axis=1
        )
        node = lax.broadcasted_iota(jnp.int32, (NODES, STEP), 0)
        return jnp.where(node == row, 1.0, 0.0).astype(BF16)

    def rows(step):
        return pl.ds(pl.multiple_of(step * STEP, STEP), STEP)

    def weight(ref, i):
        return ref[pl.ds(i * D, D), :]

    def norm(values, i):
        return layer_norm(values, norms[pl.ds(2 * i, 1), :], norms[pl.ds(2 * i + 1, 1), :])

    def loop(count, body):
        def run(step, carry):
            body(step)
            return carry

        lax.fori_loop(0, count, run, 0)

    l_grid.wait()
    spot = lax.broadcasted_iota(jnp.int32, (128, GRID), 0)
    cell = lax.broadcasted_iota(jnp.int32, (128, GRID), 1)
    wanted = jnp.where(spot < 64, 0, 60 - 1024) + lax.div(spot, 4) * 64 + lax.rem(spot, 4)
    strips[...] = dot(jnp.where(cell == wanted, 1.0, 0.0).astype(BF16), grid[...]).astype(BF16)

    sources = (
        grid.at[pl.ds(768, 256)], grid.at[pl.ds(0, 256)],
        strips.at[pl.ds(64, 64)], strips.at[pl.ds(0, 64)],
        strips.at[pl.ds(112, 16)], strips.at[pl.ds(48, 16)],
        strips.at[pl.ds(64, 16)], strips.at[pl.ds(0, 16)],
    )
    pl.semaphore_wait(barrier, len(SEGMENTS) + ROUNDS)
    halo_copies = [
        pltpu.make_async_remote_copy(
            src_ref=source,
            dst_ref=halo.at[pl.ds(first, count)],
            send_sem=halo_send.at[i],
            recv_sem=halo_recv.at[i],
            device_id=neighbour(band, sector),
            device_id_type=MESH,
        )
        for i, ((band, sector, first, count), source) in enumerate(zip(SEGMENTS, sources))
    ]
    for copy in halo_copies:
        copy.start()
    round_start(0)

    l_ge.wait()
    l_mesh.wait()
    l_wg.wait()

    def encode_first(step):
        here = rows(step)
        pos, row = pair(G_POS, step), pair(G_ROW, step)
        target = dot(onehot(row, 0, NODES), mesh[...]).astype(BF16)
        pre[here, :] = dot(ge[here, :], weight(wg, 0)) + dot(target, weight(wg, 2))
        src[here, :] = dot(onehot(pos, 0, GRID), grid[...]).astype(BF16)

    loop(3, encode_first)
    round_end(0)
    round_start(1)
    loop(2, lambda step: encode_first(step + 3))
    round_end(1)
    round_start(2)
    loop(2, lambda step: encode_first(step + 5))
    round_end(2)
    round_start(3)
    l_wm.wait()

    def node_first(step):
        here = rows(step)
        node_pre[here, :] = dot(mesh[here, :], weight(wm, 0))

    loop(2, node_first)
    total[...] = jnp.zeros((NODES, D), F32)
    for copy in halo_copies:
        copy.wait()
    round_end(3)
    round_start(4)

    def encode_last(step):
        here = rows(step)
        pos = pair(G_POS, step)
        arrived = dot(onehot(pos, GRID, HALO_PAD), halo[...]).astype(BF16)
        source = src[here, :] + arrived
        hidden = silu(pre[here, :] + dot(source, weight(wg, 1)))
        branch = norm(dot(hidden, weight(wg, 3)), 0)
        updated = (ge[here, :].astype(F32) + branch).astype(BF16)
        total[...] += dot(onehot_rows(G_ROW, step), updated)

    loop(4, encode_last)
    round_end(4)
    round_start(5)
    loop(3, lambda step: encode_last(step + 4))
    round_end(5)
    round_start(6)

    def node_last(step):
        here = rows(step)
        summed = total[here, :].astype(BF16)
        hidden = silu(node_pre[here, :] + dot(summed, weight(wm, 1)))
        branch = norm(dot(hidden, weight(wm, 2)), 1)
        mid[here, :] = (mesh[here, :].astype(F32) + branch).astype(BF16)

    loop(2, node_last)

    def near_pick(step):
        off = pair(NEAR_IDX, step)
        near_out[rows(step), :] = dot(onehot(off, 0, NODES), mid[...]).astype(BF16)

    def far_pick(step):
        off = pair(FAR_IDX, step)
        far_out[rows(step), :] = dot(onehot(off, 0, NODES), mid[...]).astype(BF16)

    loop(7, near_pick)
    round_end(6)
    near_copies = []
    for q in (0, 1, 2, 3, 5, 6, 7, 8):
        i = len(near_copies)
        near_copies.append(
            pltpu.make_async_remote_copy(
                src_ref=near_out.at[pl.ds(q * NCAP, NCAP)],
                dst_ref=near_in.at[pl.ds((8 - q) * NCAP, NCAP)],
                send_sem=near_send.at[i],
                recv_sem=near_recv.at[i],
                device_id=neighbour(q // 3 - 1, q % 3 - 1),
                device_id_type=MESH,
            )
        )
    for copy in near_copies:
        copy.start()
    loop(8, far_pick)

    slots = DEVICES // FAR_GROUPS

    def far_copy(k, g):
        other = lax.rem(me + k * FAR_MUL, DEVICES)
        return pltpu.make_async_remote_copy(
            src_ref=far_out.at[pl.ds(pl.multiple_of(other * FAR, FAR), FAR)],
            dst_ref=far_in.at[pl.ds(pl.multiple_of(k * FAR, FAR), FAR)],
            send_sem=far_send.at[g],
            recv_sem=far_recv.at[g],
            device_id=device(other),
            device_id_type=MESH,
        )

    for g in range(FAR_GROUPS):

        def send(k, carry, g=g):
            far_copy(k, g).start()
            return carry

        lax.fori_loop(max(g * slots, 1), (g + 1) * slots, send, 0)

    def far_group(g):
        first = max(g * slots, 1)
        span = pl.ds(first * FAR, ((g + 1) * slots - first) * FAR)
        return pltpu.make_async_remote_copy(
            src_ref=far_out.at[span],
            dst_ref=far_in.at[span],
            send_sem=far_send.at[g],
            recv_sem=far_recv.at[g],
            device_id=device(lax.rem(me + 1, DEVICES)),
            device_id_type=MESH,
        )

    l_wp.wait()
    l_pe.wait()

    def process_first(step):
        here = rows(step)
        pos, row = pair(P_POS, step), pair(P_ROW, step)
        target = dot(onehot(row, 0, NODES), mid[...]).astype(BF16)
        pre[here, :] = dot(pe[here, :], weight(wp, 0)) + dot(target, weight(wp, 2))
        src[here, :] = dot(onehot(pos, 0, NODES), mid[...]).astype(BF16)

    loop(8, process_first)
    l_wr.wait()

    def grid_step(step):
        here = rows(step)
        cells = grid[here, :]
        hidden = silu(dot(cells, weight(wr, 0)))
        branch = norm(dot(hidden, weight(wr, 1)), 2)
        gout[here, :] = (cells.astype(F32) + branch).astype(BF16)

    loop(4, grid_step)
    store_grid = pltpu.make_async_copy(gout, grid_out, store_sem.at[0])
    store_grid.start()
    l_wn.wait()

    def out_first(step):
        here = rows(step)
        node_pre[here, :] = dot(mid[here, :], weight(wn, 0))

    loop(2, out_first)
    total[...] = jnp.zeros((NODES, D), F32)

    for copy in near_copies:
        copy.wait()

    def take_near(step):
        here = rows(step)
        off = pair(P_POS, step)
        src[here, :] += dot(onehot(off, NODES, NEAR_PAD), near_in[...]).astype(BF16)

    loop(8, take_near)

    for g in range(FAR_GROUPS - 1):
        far_group(g).wait()

        def take_far(step, g=g):
            here = rows(step)
            off = pair(P_POS, step)
            table = far_in[pl.ds(g * slots * FAR, slots * FAR), :]
            hot = onehot(off, NODES + NEAR_PAD + g * slots * FAR, slots * FAR)
            src[here, :] += dot(hot, table).astype(BF16)

        loop(8, take_far)

    far_group(FAR_GROUPS - 1).wait()

    def process_last(step):
        here = rows(step)
        off = pair(P_POS, step)
        base = (FAR_GROUPS - 1) * slots * FAR
        table = far_in[pl.ds(base, slots * FAR), :]
        hot = onehot(off, NODES + NEAR_PAD + base, slots * FAR)
        source = src[here, :] + dot(hot, table).astype(BF16)
        hidden = silu(pre[here, :] + dot(source, weight(wp, 1)))
        branch = norm(dot(hidden, weight(wp, 3)), 3)
        updated = (pe[here, :].astype(F32) + branch).astype(BF16)
        total[...] += dot(onehot_rows(P_ROW, step), updated)

    loop(8, process_last)

    def out_last(step):
        here = rows(step)
        summed = total[here, :].astype(BF16)
        hidden = silu(node_pre[here, :] + dot(summed, weight(wn, 1)))
        branch = norm(dot(hidden, weight(wn, 2)), 4)
        mout[here, :] = (mid[here, :].astype(F32) + branch).astype(BF16)

    loop(2, out_last)
    store_mesh = pltpu.make_async_copy(mout, mesh_out, store_sem.at[1])
    store_mesh.start()
    store_mesh.wait()
    store_grid.wait()


def grid_spots(sender):
    i, j = sender // 72, sender % 72
    north, south = i < HW, i >= 20
    west, east = j < HW, j >= 68
    band = jnp.where(north, i, jnp.where(south, i - 20, i - HW))
    sector = jnp.where(west, j, jnp.where(east, j - 68, j - HW))
    edge = north | south
    side = west | east
    base = jnp.where(
        edge,
        jnp.where(
            side,
            1664 + 16 * (2 * south.astype(jnp.int32) + east.astype(jnp.int32)),
            jnp.where(north, 1024, 1280),
        ),
        jnp.where(west, 1536, jnp.where(east, 1600, 0)),
    )
    return base + band * jnp.where(side, 4, 64) + sector


def source_spots(sender, me):
    far = sender - (NODES + NEAR)
    other, slot = far // FAR, far % FAR
    place = ((me - other + DEVICES) * FAR_INV) % DEVICES
    return jnp.where(far >= 0, NODES + NEAR_PAD + place * FAR + slot, sender)


def node_rows(receiver, window):
    return jnp.where(receiver >= 0, window[:, None] * 128 + receiver, -1)


def body(
    grid_nodes, mesh_nodes, g2m_edges, mesh_edges, g2m_sender, g2m_receiver, g2m_window,
    mesh_sender, mesh_receiver, mesh_window, near_rows, far_rows,
    w_g2m_edge, w_mesh_node, w_grid_node, w_proc_edge, w_proc_node, norms,
):
    me = lax.axis_index("lat") * 16 + lax.axis_index("lon")
    near = jnp.concatenate(
        [near_rows.reshape(-1), jnp.full((NEAR_PAD - NEAR,), -1, jnp.int32)]
    ).reshape(-1, 128)
    idx = jnp.concatenate(
        [
            grid_spots(g2m_sender),
            node_rows(g2m_receiver, g2m_window),
            source_spots(mesh_sender, me),
            node_rows(mesh_receiver, mesh_window),
            near,
            far_rows.reshape(-1, 128),
        ],
        axis=0,
    )
    vmem = pl.BlockSpec(memory_space=pltpu.VMEM)
    any_space = pl.BlockSpec(memory_space=pl.ANY)

    def buf(count, dtype=BF16):
        return pltpu.VMEM((count, D), dtype)

    dma = pltpu.SemaphoreType.DMA
    mesh_out, grid_out = pl.pallas_call(
        kernel,
        out_shape=(
            jax.ShapeDtypeStruct((NODES, D), BF16),
            jax.ShapeDtypeStruct((GRID, D), BF16),
        ),
        in_specs=[vmem, vmem] + [any_space] * 9,
        out_specs=(any_space, any_space),
        scratch_shapes=[
            buf(GRID), buf(HALO_PAD), buf(128), buf(NODES), buf(G_EDGES), buf(P_EDGES),
            buf(4 * D), buf(3 * D), buf(2 * D), buf(4 * D), buf(3 * D),
            buf(P_EDGES, F32), buf(P_EDGES), buf(NODES, F32), buf(NODES, F32), buf(NODES),
            buf(NEAR_PAD), buf(NEAR_PAD), buf(DEVICES * FAR), buf(DEVICES * FAR),
            buf(GRID), buf(NODES),
            dma((9,)), dma((2,)), dma((8,)), dma((8,)), dma((8,)), dma((8,)),
            dma((FAR_GROUPS,)), dma((FAR_GROUPS,)), pltpu.SemaphoreType.REGULAR((ROUNDS,)),
        ],
        compiler_params=pltpu.CompilerParams(
            collective_id=0, has_side_effects=True, vmem_limit_bytes=52 * 2**20
        ),
    )(
        idx, norms.reshape(10, D),
        grid_nodes.reshape(GRID, D), mesh_nodes, g2m_edges.reshape(-1, D), mesh_edges.reshape(-1, D),
        w_g2m_edge.reshape(-1, D), w_mesh_node.reshape(-1, D), w_grid_node.reshape(-1, D),
        w_proc_edge.reshape(-1, D), w_proc_node.reshape(-1, D),
    )
    return mesh_out, grid_out.reshape(grid_nodes.shape)


def solution(mesh):
    both = ("lat", "lon")
    return jax.shard_map(
        body,
        mesh=mesh,
        in_specs=(
            P("lat", "lon", None), P(both, None), P(both, None, None), P(both, None, None),
            P(both, None), P(both, None), P(both), P(both, None), P(both, None), P(both),
            P(both, None, None), P(both, None, None),
            P(), P(), P(), P(), P(), P(),
        ),
        out_specs=(P(both, None), P("lat", "lon", None)),
        check_vma=False,
    )
```

time: 177 us -> 106 us (0.60)
  the two profiles are of different devices: /device:TPU:1 before, /device:TPU:3 now
where the time goes in v1:
time: 106 us; the launch traced here: 105 us
  Pallas kernels  94.6 us (89%)
  local copies, waits for them, and re-layouts  6.4 us (6%)
  other arithmetic  3.62 us (3%)
    pallas_call x1, Pallas kernels, body(): pl.pallas_call(kernel, out_shape=(jax.ShapeDtypeStruct((NODES, D), BF16),...  94.6 us
    unnamed x5, local copies, waits for them, and re-layouts  4.92 us

profile of v1, /device:TPU:3, one launch (start us, length us, event | category | flops | bytes accessed | tf_op | source)
XLA Modules:
  0.0 105.3 jit_solution(11460059940869926980)
XLA Ops:
  0.6 0.7 broadcast_multiply_fusion.1
  1.3 0.7 broadcast_multiply_fusion
  2.0 0.8 fusion.7
  2.7 0.8 add_select_fusion.6
  3.5 0.7 reduce
  4.3 0.1 reshape.47
  4.3 0.7 reshape.50.norms
  5.1 0.8 copy.21
  5.9 0.1 reshape.49
  6.0 0.6 concatenate.7.idx
  6.5 0.0 copy-start
  6.6 1.0 copy-done
  7.6 94.6 %shard_map.185 = (bf16[512,512]{1,0:T(8,128)(2,1)S(1)}, bf16[1024,512]{1,0:T(8,128)(2,1)}) custom-call(s32[90,128]{1,0:T(8,128)S(1)} %concatenate.7.idx, f32[10,512]{1,0:T(8,128)S(1)} %reshape.50.norms, bf16[1024,512]{1,0:T(8,128)(2,1)} %bitcast.18, bf16[512,512]{1,0:T(8,128)(2,1)S(1)} %copy-done, bf16[1792,512]{1,0:T(8,128)(2,1)} %bitcast.14, ...), custom_call_target="tpu_custom_call" | custom-call | tf_op jit(solution)/shard_map/pallas_call | solution.py:439
  102.2 0.8 copy.24
  103.0 2.3 %copy.25 = bf16[16,64,512]{2,1,0:T(8,128)(2,1)} copy(bf16[16,64,512]{2,1,0:T(8,128)(2,1)} %bitcast.17) | data formatting | bytes 2097152
  (1 shorter events, 0.0 us)
Async XLA Ops:
  6.5 1.0 copy-start

commit v2 on v1

v2 whole, which is shorter than its diff:
```python
import jax
import jax.numpy as jnp
from jax import lax
from jax.experimental import pallas as pl
from jax.experimental.pallas import tpu as pltpu
from jax.sharding import PartitionSpec as P

HW = 4
EPS = 1e-05
D = 512
BF16 = jnp.bfloat16
F32 = jnp.float32
MESH = pl.DeviceIdType.MESH

GRID = 1024
HALO = 704
HALO_PAD = 768
NODES = 512
NCAP = 192
NEAR = 9 * NCAP
NEAR_ORDER = (1, 7, 3, 5, 0, 2, 6, 8)
NEAR_ROWS = 8 * NCAP
NEAR_GROUPS = ((0, 2), (2, 4), (4, 8))
FAR = 16
DEVICES = 128
G_EDGES = 1792
P_EDGES = 2048
E_STEP = 896
P_STEP = 1024
N_STEP = 512
C_STEP = 512
F_STEP = 1024

G_POS, G_ROW, P_POS, P_ROW = 0, 16, 32, 48
G_BLOCKS, P_BLOCKS = 14, 16

FAR_MUL = 77
FAR_INV = 5
FAR_GROUPS = 2
HOP = 12
HOPS = 10

SEGMENTS = (
    (1, 0, 0, 256),
    (-1, 0, 256, 256),
    (0, 1, 512, 64),
    (0, -1, 576, 64),
    (1, 1, 640, 16),
    (1, -1, 656, 16),
    (-1, 1, 672, 16),
    (-1, -1, 688, 16),
)


def dot(a, b):
    return jnp.dot(a, b, preferred_element_type=F32)


def silu(v):
    half = 0.5 * v
    return (half + half * jnp.tanh(half)).astype(BF16)


def layer_norm(values, gain, shift):
    mean = jnp.mean(values, axis=-1, keepdims=True)
    centred = values - mean
    variance = jnp.mean(centred * centred, axis=-1, keepdims=True)
    return centred * lax.rsqrt(variance + EPS) * gain + shift


def grid_spots(sender):
    i = (sender * 14564) >> 20
    j = sender - 72 * i
    north, south = i < HW, i >= 20
    west, east = j < HW, j >= 68
    edge, side = north | south, west | east
    band = jnp.where(north, i, jnp.where(south, i - 20, i - HW))
    sector = jnp.where(west, j, jnp.where(east, j - 68, j - HW))
    corner = 1664 + jnp.where(south, 32, 0) + jnp.where(east, 16, 0)
    base = jnp.where(
        edge,
        jnp.where(side, corner, jnp.where(north, 1024, 1280)),
        jnp.where(west, 1536, jnp.where(east, 1600, 0)),
    )
    return base + band * jnp.where(side, 4, 64) + sector


def source_spots(sender, me):
    far = sender - (NODES + NEAR)
    place = (((me - (far >> 4)) & (DEVICES - 1)) * FAR_INV) & (DEVICES - 1)
    near = sender - NODES
    q = (near * 10923) >> 21
    order = jnp.zeros_like(q)
    for i, position in enumerate(NEAR_ORDER):
        order = jnp.where(q == position, i, order)
    near_spot = NODES + order * NCAP + near - q * NCAP
    far_spot = NODES + NEAR_ROWS + place * FAR + (far & (FAR - 1))
    return jnp.where(far >= 0, far_spot, jnp.where(near >= 0, near_spot, sender))


def kernel(
    g_window, p_window,
    gs_h, gr_h, ps_h, pr_h, near_h, far_h, norms_h,
    grid_h, mesh_h, ge_h, pe_h, wg_h, wm_h, wr_h, wp_h, wn_h,
    mesh_out, grid_out,
    gs, gr, ps, pr, near, far, norms, idx,
    grid, halo, strips, mesh, ge, pe, wg, wm, wr, wp, wn,
    pre, src, total, node_pre, mid, near_out, near_in, far_out, far_in, gout, mout,
    far_hot, table,
    load_sem, store_sem, halo_send, halo_recv, near_send, near_recv, far_send, far_recv, round_sem,
):
    lat, lon = lax.axis_index("lat"), lax.axis_index("lon")
    me = lat * 16 + lon

    def device(p):
        return (lax.div(p, 16), lax.rem(p, 16))

    def neighbour(band, sector):
        return (lax.rem(lat + band + 8, 8), lax.rem(lon + sector + 16, 16))

    loads = [
        pltpu.make_async_copy(h, v, load_sem.at[i])
        for i, (h, v) in enumerate(
            ((grid_h, grid), (gs_h, gs), (gr_h, gr), (mesh_h, mesh), (ge_h, ge), (wg_h, wg),
             (ps_h, ps), (pr_h, pr), (near_h, near), (far_h, far), (norms_h, norms), (wm_h, wm),
             (wp_h, wp), (pe_h, pe), (wr_h, wr), (wn_h, wn))
        )
    ]
    for copy in loads:
        copy.start()
    l_grid, l_gs, l_gr, l_mesh, l_ge, l_wg = loads[:6]
    l_small, (l_wm, l_wp, l_pe, l_wr, l_wn) = loads[6:11], loads[11:]

    halo[pl.ds(HALO, HALO_PAD - HALO), :] = jnp.zeros((HALO_PAD - HALO, D), BF16)
    far_in[pl.ds(0, FAR), :] = jnp.zeros((FAR, D), BF16)

    barrier = pltpu.get_barrier_semaphore()

    def greet(to):
        pl.semaphore_signal(barrier, inc=1, device_id=to, device_id_type=MESH)

    for band, sector, _, _ in SEGMENTS:
        greet(neighbour(band, sector))
    steps_back = [HOP * j for j in range(1, HOPS + 1)] + list(range(1, HOP))
    for back in steps_back:
        greet(device(lax.rem(me + DEVICES - back, DEVICES)))

    lane = lax.broadcasted_iota(jnp.int32, (128, 128), 1)

    def offsets(first, b):
        row = idx[pl.ds(first + b, 1), :]
        return jnp.broadcast_to(row, (128, 128)).T - lane

    def columns(first, step, count):
        blocks = count // 128
        return jnp.concatenate([offsets(first, step * blocks + b) for b in range(blocks)], axis=0)

    def node_rows(receiver, window, first, count):
        for b in range(count):
            row = receiver[pl.ds(b, 1), :]
            idx[pl.ds(first + b, 1), :] = jnp.where(row >= 0, row + 128 * window[b], -1)

    def onehot(off, base, count):
        return jnp.concatenate(
            [jnp.where(off == base + 128 * k, 1.0, 0.0).astype(BF16) for k in range(count // 128)],
            axis=1,
        )

    def onehot_rows(first, step, count):
        blocks = count // 128
        row = jnp.concatenate(
            [idx[pl.ds(first + step * blocks + b, 1), :] for b in range(blocks)], axis=1
        )
        node = lax.broadcasted_iota(jnp.int32, (NODES, count), 0)
        return jnp.where(node == row, 1.0, 0.0).astype(BF16)

    def rows(step, count):
        return pl.ds(pl.multiple_of(step * count, count), count)

    def weight(ref, i):
        return ref[pl.ds(i * D, D), :]

    def norm(values, i):
        return layer_norm(values, norms[i, pl.ds(0, 1), :], norms[i, pl.ds(1, 1), :])

    def loop(count, body):
        def run(step, carry):
            body(step)
            return carry

        lax.fori_loop(0, count, run, 0)

    l_grid.wait()
    spot = lax.broadcasted_iota(jnp.int32, (128, GRID), 0)
    cell = lax.broadcasted_iota(jnp.int32, (128, GRID), 1)
    wanted = jnp.where(spot < 64, 0, 60 - 1024) + lax.div(spot, 4) * 64 + lax.rem(spot, 4)
    strips[...] = dot(jnp.where(cell == wanted, 1.0, 0.0).astype(BF16), grid[...]).astype(BF16)

    sources = (
        grid.at[pl.ds(768, 256)], grid.at[pl.ds(0, 256)],
        strips.at[pl.ds(64, 64)], strips.at[pl.ds(0, 64)],
        strips.at[pl.ds(112, 16)], strips.at[pl.ds(48, 16)],
        strips.at[pl.ds(64, 16)], strips.at[pl.ds(0, 16)],
    )
    pl.semaphore_wait(barrier, len(SEGMENTS) + len(steps_back))
    halo_copies = [
        pltpu.make_async_remote_copy(
            src_ref=source,
            dst_ref=halo.at[pl.ds(first, count)],
            send_sem=halo_send.at[i],
            recv_sem=halo_recv.at[i],
            device_id=neighbour(band, sector),
            device_id_type=MESH,
        )
        for i, ((band, sector, first, count), source) in enumerate(zip(SEGMENTS, sources))
    ]
    for copy in halo_copies:
        copy.start()
    for ahead in range(1, HOP):
        pl.semaphore_signal(
            round_sem, inc=1, device_id=device(lax.rem(me + ahead, DEVICES)), device_id_type=MESH
        )

    l_gs.wait()
    l_gr.wait()
    idx[pl.ds(G_POS, G_BLOCKS), :] = grid_spots(gs[...])
    node_rows(gr, g_window, G_ROW, G_BLOCKS)
    l_ge.wait()
    l_mesh.wait()
    l_wg.wait()

    def encode_first(step):
        here = rows(step, E_STEP)
        row = columns(G_ROW, step, E_STEP)
        target = dot(onehot(row, 0, NODES), mesh[...]).astype(BF16)
        pos = columns(G_POS, step, E_STEP)
        source = dot(onehot(pos, 0, GRID), grid[...]).astype(BF16)
        pre[here, :] = (
            dot(ge[here, :], weight(wg, 0)) + dot(target, weight(wg, 2)) + dot(source, weight(wg, 1))
        )

    loop(G_EDGES // E_STEP, encode_first)
    for copy in l_small:
        copy.wait()
    idx[pl.ds(P_POS, P_BLOCKS), :] = source_spots(ps[...], me)
    node_rows(pr, p_window, P_ROW, P_BLOCKS)

    edge = lax.broadcasted_iota(jnp.int32, (F_STEP, DEVICES), 0)
    lane_of = lax.broadcasted_iota(jnp.int32, (F_STEP, DEVICES), 1)
    of_slot = jnp.where(
        (lax.broadcasted_iota(jnp.int32, (F_STEP, FAR), 0) & (FAR - 1))
        == lax.broadcasted_iota(jnp.int32, (F_STEP, FAR), 1), 1.0, 0.0
    )
    spread = jnp.ones((FAR, 128), BF16)

    def far_spots(step):
        of_list = jnp.where((edge >> 4) + step * (F_STEP // FAR) == lane_of, 1.0, 0.0).astype(BF16)

        def expand(part):
            mine = lax.dot_general(
                of_list, part.astype(F32).astype(BF16), (((1,), (1,)), ((), ())),
                preferred_element_type=F32,
            )
            return dot((mine * of_slot).astype(BF16), spread)

        lists = far[0]
        off = 16.0 * expand(lists >> 4) + expand(lists & 15) - lane_of.astype(F32)
        far_hot[rows(step, F_STEP), :] = jnp.concatenate(
            [jnp.where(off == 128.0 * k, 1.0, 0.0).astype(BF16) for k in range(NODES // 128)], axis=1
        )

    loop(DEVICES * FAR // F_STEP, far_spots)
    l_wm.wait()

    def node_first(step):
        here = rows(step, N_STEP)
        node_pre[here, :] = dot(mesh[here, :], weight(wm, 0))

    loop(NODES // N_STEP, node_first)
    total[...] = jnp.zeros((NODES, D), F32)
    for copy in halo_copies:
        copy.wait()

    table[pl.ds(0, HALO_PAD), :] = dot(halo[...], weight(wg, 1)).astype(BF16)

    def encode_last(step):
        here = rows(step, E_STEP)
        pos = columns(G_POS, step, E_STEP)
        hidden = silu(pre[here, :] + dot(onehot(pos, GRID, HALO_PAD), table[pl.ds(0, HALO_PAD), :]))
        branch = norm(dot(hidden, weight(wg, 3)), 0)
        updated = (ge[here, :].astype(F32) + branch).astype(BF16)
        total[...] += dot(onehot_rows(G_ROW, step, E_STEP), updated)

    loop(G_EDGES // E_STEP, encode_last)

    def node_last(step):
        here = rows(step, N_STEP)
        summed = total[here, :].astype(BF16)
        hidden = silu(node_pre[here, :] + dot(summed, weight(wm, 1)))
        branch = norm(dot(hidden, weight(wm, 2)), 1)
        mid[here, :] = (mesh[here, :].astype(F32) + branch).astype(BF16)

    loop(NODES // N_STEP, node_last)

    def far_pick(step):
        here = rows(step, F_STEP)
        far_out[here, :] = dot(far_hot[here, :], mid[...]).astype(BF16)

    loop(DEVICES * FAR // F_STEP, far_pick)
    pl.semaphore_wait(round_sem, HOP - 1)

    slots = DEVICES // FAR_GROUPS

    def far_copy(k, g):
        other = lax.rem(me + k * FAR_MUL, DEVICES)
        return pltpu.make_async_remote_copy(
            src_ref=far_out.at[pl.ds(pl.multiple_of(other * FAR, FAR), FAR)],
            dst_ref=far_in.at[pl.ds(pl.multiple_of(k * FAR, FAR), FAR)],
            send_sem=far_send.at[g],
            recv_sem=far_recv.at[g],
            device_id=device(other),
            device_id_type=MESH,
        )

    for g in range(FAR_GROUPS):

        def send(k, carry, g=g):
            far_copy(k, g).start()
            return carry

        lax.fori_loop(max(g * slots, 1), (g + 1) * slots, send, 0)

    def near_columns(q):
        row = near[q]
        first = jnp.broadcast_to(row[:, :128], (128, 128)).T - lane
        second = jnp.broadcast_to(row[:, 64:], (128, 128)).T - lane
        return jnp.concatenate([first, second[64:]], axis=0)

    def near_pick(half):
        off = jnp.concatenate([near_columns(5 * half + i) for i in range(4)], axis=0)
        picked = dot(onehot(off, 0, NODES), mid[...]).astype(BF16)
        near_out[pl.ds(pl.multiple_of(half * 4 * NCAP, 4 * NCAP), 4 * NCAP), :] = picked

    loop(2, near_pick)
    near_copies = []
    for i, q in enumerate(NEAR_ORDER):
        own = 8 - q
        near_copies.append(
            pltpu.make_async_remote_copy(
                src_ref=near_out.at[pl.ds((own - own // 5) * NCAP, NCAP)],
                dst_ref=near_in.at[pl.ds(i * NCAP, NCAP)],
                send_sem=near_send.at[i],
                recv_sem=near_recv.at[i],
                device_id=neighbour(own // 3 - 1, own % 3 - 1),
                device_id_type=MESH,
            )
        )
    for copy in near_copies:
        copy.start()

    def far_group(g):
        first = max(g * slots, 1)
        span = pl.ds(first * FAR, ((g + 1) * slots - first) * FAR)
        return pltpu.make_async_remote_copy(
            src_ref=far_out.at[span],
            dst_ref=far_in.at[span],
            send_sem=far_send.at[g],
            recv_sem=far_recv.at[g],
            device_id=device(lax.rem(me + 1, DEVICES)),
            device_id_type=MESH,
        )

    l_wp.wait()
    l_pe.wait()

    def process_first(step):
        here = rows(step, P_STEP)
        pos, row = columns(P_POS, step, P_STEP), columns(P_ROW, step, P_STEP)
        target = dot(onehot(row, 0, NODES), mid[...]).astype(BF16)
        pre[here, :] = dot(pe[here, :], weight(wp, 0)) + dot(target, weight(wp, 2))
        src[here, :] = dot(onehot(pos, 0, NODES), mid[...]).astype(BF16)

    loop(P_EDGES // P_STEP, process_first)
    l_wr.wait()

    def grid_step(step):
        here = rows(step, C_STEP)
        cells = grid[here, :]
        hidden = silu(dot(cells, weight(wr, 0)))
        branch = norm(dot(hidden, weight(wr, 1)), 2)
        gout[here, :] = (cells.astype(F32) + branch).astype(BF16)

    loop(GRID // C_STEP, grid_step)
    store_grid = pltpu.make_async_copy(gout, grid_out, store_sem.at[0])
    store_grid.start()
    l_wn.wait()

    def out_first(step):
        here = rows(step, N_STEP)
        node_pre[here, :] = dot(mid[here, :], weight(wn, 0))

    loop(NODES // N_STEP, out_first)
    total[...] = jnp.zeros((NODES, D), F32)

    far_base = NODES + NEAR_ROWS

    def take(count, base, arrived):
        def step_of(step):
            here = rows(step, P_STEP)
            off = columns(P_POS, step, P_STEP)
            src[here, :] += dot(onehot(off, base, count), arrived[...]).astype(BF16)

        loop(P_EDGES // P_STEP, step_of)

    def near_part(group):
        first, last = group
        for copy in near_copies[first:last]:
            copy.wait()
        return pl.ds(first * NCAP, (last - first) * NCAP)

    for g in range(FAR_GROUPS):
        far_group(g).wait()
        first = g * slots * FAR
        take(slots * FAR, far_base + first, far_in.at[pl.ds(first, slots * FAR)])
    for group in NEAR_GROUPS[:-1]:
        part = near_part(group)
        take(part.size, NODES + part.start, near_in.at[part])

    def project(step):
        here = rows(step, P_STEP)
        pre[here, :] += dot(src[here, :], weight(wp, 1))

    loop(P_EDGES // P_STEP, project)
    last = near_part(NEAR_GROUPS[-1])
    table[...] = dot(near_in[last, :], weight(wp, 1)).astype(BF16)

    def process_last(step):
        here = rows(step, P_STEP)
        off = columns(P_POS, step, P_STEP)
        hidden = silu(pre[here, :] + dot(onehot(off, NODES + last.start, last.size), table[...]))
        branch = norm(dot(hidden, weight(wp, 3)), 3)
        updated = (pe[here, :].astype(F32) + branch).astype(BF16)
        total[...] += dot(onehot_rows(P_ROW, step, P_STEP), updated)

    loop(P_EDGES // P_STEP, process_last)

    def out_last(step):
        here = rows(step, N_STEP)
        summed = total[here, :].astype(BF16)
        hidden = silu(node_pre[here, :] + dot(summed, weight(wn, 1)))
        branch = norm(dot(hidden, weight(wn, 2)), 4)
        mout[here, :] = (mid[here, :].astype(F32) + branch).astype(BF16)

    loop(NODES // N_STEP, out_last)
    store_mesh = pltpu.make_async_copy(mout, mesh_out, store_sem.at[1])
    store_mesh.start()
    store_mesh.wait()
    store_grid.wait()


def body(
    grid_nodes, mesh_nodes, g2m_edges, mesh_edges, g2m_sender, g2m_receiver, g2m_window,
    mesh_sender, mesh_receiver, mesh_window, near_rows, far_rows,
    w_g2m_edge, w_mesh_node, w_grid_node, w_proc_edge, w_proc_node, norms,
):
    smem = pl.BlockSpec(memory_space=pltpu.SMEM)
    any_space = pl.BlockSpec(memory_space=pl.ANY)

    def buf(count, dtype=BF16):
        return pltpu.VMEM((count, D), dtype)

    def ints(*shape):
        return pltpu.VMEM(shape, jnp.int32)

    dma = pltpu.SemaphoreType.DMA
    mesh_out, grid_out = pl.pallas_call(
        kernel,
        out_shape=(
            jax.ShapeDtypeStruct((NODES, D), BF16),
            jax.ShapeDtypeStruct((GRID, D), BF16),
        ),
        in_specs=[smem, smem] + [any_space] * 16,
        out_specs=(any_space, any_space),
        scratch_shapes=[
            ints(G_BLOCKS, 128), ints(G_BLOCKS, 128), ints(P_BLOCKS, 128), ints(P_BLOCKS, 128),
            ints(9, 1, NCAP), ints(1, FAR, DEVICES), pltpu.VMEM((5, 2, D), F32), ints(64, 128),
            buf(GRID), buf(HALO_PAD), buf(128), buf(NODES), buf(G_EDGES), buf(P_EDGES),
            buf(4 * D), buf(3 * D), buf(2 * D), buf(4 * D), buf(3 * D),
            buf(P_EDGES, F32), buf(P_EDGES), buf(NODES, F32), buf(NODES, F32), buf(NODES),
            buf(NEAR_ROWS), buf(NEAR_ROWS), buf(DEVICES * FAR), buf(DEVICES * FAR),
            buf(GRID), buf(NODES), buf(DEVICES * FAR), buf(HALO_PAD),
            dma((16,)), dma((2,)), dma((8,)), dma((8,)), dma((8,)), dma((8,)),
            dma((FAR_GROUPS,)), dma((FAR_GROUPS,)), pltpu.SemaphoreType.REGULAR,
        ],
        compiler_params=pltpu.CompilerParams(
            collective_id=0, has_side_effects=True, vmem_limit_bytes=63 * 2**20
        ),
    )(
        g2m_window, mesh_window,
        g2m_sender, g2m_receiver, mesh_sender, mesh_receiver, near_rows.transpose(1, 0, 2), far_rows.transpose(0, 2, 1), norms,
        grid_nodes.reshape(GRID, D), mesh_nodes, g2m_edges.reshape(-1, D), mesh_edges.reshape(-1, D),
        w_g2m_edge.reshape(-1, D), w_mesh_node.reshape(-1, D), w_grid_node.reshape(-1, D),
        w_proc_edge.reshape(-1, D), w_proc_node.reshape(-1, D),
    )
    return mesh_out, grid_out.reshape(grid_nodes.shape)


def solution(mesh):
    both = ("lat", "lon")
    return jax.shard_map(
        body,
        mesh=mesh,
        in_specs=(
            P("lat", "lon", None), P(both, None), P(both, None, None), P(both, None, None),
            P(both, None), P(both, None), P(both), P(both, None), P(both, None), P(both),
            P(both, None, None), P(both, None, None),
            P(), P(), P(), P(), P(), P(),
        ),
        out_specs=(P(both, None), P("lat", "lon", None)),
        check_vma=False,
    )
```

time: 106 us -> 78.7 us (0.74)
  the two profiles are of different devices: /device:TPU:3 before, /device:TPU:1 now
where the time goes in v2:
time: 78.7 us; the launch traced here: 78.5 us
  Pallas kernels  73.7 us (94%)
  local copies, waits for them, and re-layouts  4.16 us (5%)
    pallas_call x1, Pallas kernels, body(): pl.pallas_call(kernel, out_shape=(jax.ShapeDtypeStruct((NODES, D), BF16),...  73.7 us
    unnamed x2, local copies, waits for them, and re-layouts  4.16 us

profile of v2, /device:TPU:1, one launch (start us, length us, event | category | flops | bytes accessed | tf_op | source)
XLA Modules:
  0.0 78.5 jit_solution(9852708692305805387)
XLA Ops:
  0.6 73.7 %shard_map.185 = (bf16[512,512]{1,0:T(8,128)(2,1)}, bf16[1024,512]{1,0:T(8,128)(2,1)}) custom-call(s32[14]{0:T(128)} %g_window.1, s32[16]{0:T(128)} %p_window.1, s32[14,128]{1,0:T(8,128)} %gs_h.1, s32[14,128]{1,0:T(8,128)} %gr_h.1, s32[16,128]{1,0:T(8,128)} %ps_h.1, s32[16,128]{1,0:T(8,128)} %pr_h.1, s32[9,1,192]{2,1,0:T(1,128)} %bitcast.20, ...), custom_call_target="tpu_custom_call" | custom-call | tf_op jit(solution)/shard_map/pallas_call | solution.py:476
  74.4 1.9 %copy.22 = bf16[512,512]{1,0:T(8,128)(2,1)} copy(bf16[512,512]{1,0:T(8,128)(2,1)} %get-tuple-element.8) | data formatting | bytes 1048576
  76.2 2.3 %copy.23 = bf16[16,64,512]{2,1,0:T(8,128)(2,1)} copy(bf16[16,64,512]{2,1,0:T(8,128)(2,1)} %bitcast.17) | data formatting | bytes 2097152

commit v3 on v2

--- a/solution.py
+++ b/solution.py
@@ -20,13 +20,14 @@
 NEAR = 9 * NCAP
 NEAR_ORDER = (1, 7, 3, 5, 0, 2, 6, 8)
 NEAR_ROWS = 8 * NCAP
-NEAR_GROUPS = ((0, 2), (2, 4), (4, 8))
+NEAR_GROUPS = ((0, 2), (2, 6), (6, 8))
+LAST = (NEAR_GROUPS[-1][1] - NEAR_GROUPS[-1][0]) * NCAP
 FAR = 16
 DEVICES = 128
 G_EDGES = 1792
 P_EDGES = 2048
-E_STEP = 896
-P_STEP = 1024
+E_STEP = 1792
+P_STEP = 2048
 N_STEP = 512
 C_STEP = 512
 F_STEP = 1024
@@ -105,9 +106,9 @@
     mesh_out, grid_out,
     gs, gr, ps, pr, near, far, norms, idx,
     grid, halo, strips, mesh, ge, pe, wg, wm, wr, wp, wn,
-    pre, src, total, node_pre, mid, near_out, near_in, far_out, far_in, gout, mout,
-    far_hot, table,
-    load_sem, store_sem, halo_send, halo_recv, near_send, near_recv, far_send, far_recv, round_sem,
+    pre, src, total, node_pre, mid, near_out, near_in, far_out, far_in,
+    far_hot, table, cells, last_hot, sum_hot,
+    load_sem, halo_send, halo_recv, near_send, near_recv, far_send, far_recv, round_sem,
 ):
     lat, lon = lax.axis_index("lat"), lax.axis_index("lon")
     me = lat * 16 + lon
@@ -229,14 +230,17 @@
     l_mesh.wait()
     l_wg.wait()
 
+    table[pl.ds(0, NODES), :] = dot(mesh[...], weight(wg, 2)).astype(BF16)
+    cells[...] = dot(grid[...], weight(wg, 1)).astype(BF16)
+
     def encode_first(step):
         here = rows(step, E_STEP)
         row = columns(G_ROW, step, E_STEP)
-        target = dot(onehot(row, 0, NODES), mesh[...]).astype(BF16)
         pos = columns(G_POS, step, E_STEP)
-        source = dot(onehot(pos, 0, GRID), grid[...]).astype(BF16)
         pre[here, :] = (
-            dot(ge[here, :], weight(wg, 0)) + dot(target, weight(wg, 2)) + dot(source, weight(wg, 1))
+            dot(ge[here, :], weight(wg, 0))
+            + dot(onehot(row, 0, NODES), table[pl.ds(0, NODES), :])
+            + dot(onehot(pos, 0, GRID), cells[...])
         )
 
     loop(G_EDGES // E_STEP, encode_first)
@@ -254,7 +258,8 @@
     spread = jnp.ones((FAR, 128), BF16)
 
     def far_spots(step):
-        of_list = jnp.where((edge >> 4) + step * (F_STEP // FAR) == lane_of, 1.0, 0.0).astype(BF16)
+        place = (edge >> 4) + step * (F_STEP // FAR)
+        of_list = jnp.where(((me + place * FAR_MUL) & (DEVICES - 1)) == lane_of, 1.0, 0.0).astype(BF16)
 
         def expand(part):
             mine = lax.dot_general(
@@ -306,23 +311,23 @@
         here = rows(step, F_STEP)
         far_out[here, :] = dot(far_hot[here, :], mid[...]).astype(BF16)
 
-    loop(DEVICES * FAR // F_STEP, far_pick)
-    pl.semaphore_wait(round_sem, HOP - 1)
-
     slots = DEVICES // FAR_GROUPS
 
     def far_copy(k, g):
-        other = lax.rem(me + k * FAR_MUL, DEVICES)
+        there = pl.ds(pl.multiple_of(k * FAR, FAR), FAR)
         return pltpu.make_async_remote_copy(
-            src_ref=far_out.at[pl.ds(pl.multiple_of(other * FAR, FAR), FAR)],
-            dst_ref=far_in.at[pl.ds(pl.multiple_of(k * FAR, FAR), FAR)],
+            src_ref=far_out.at[there],
+            dst_ref=far_in.at[there],
             send_sem=far_send.at[g],
             recv_sem=far_recv.at[g],
-            device_id=device(other),
+            device_id=device(lax.rem(me + k * FAR_MUL, DEVICES)),
             device_id_type=MESH,
         )
 
     for g in range(FAR_GROUPS):
+        far_pick(g)
+        if g == 0:
+            pl.semaphore_wait(round_sem, HOP - 1)
 
         def send(k, carry, g=g):
             far_copy(k, g).start()
@@ -385,14 +390,14 @@
 
     def grid_step(step):
         here = rows(step, C_STEP)
-        cells = grid[here, :]
-        hidden = silu(dot(cells, weight(wr, 0)))
+        own = grid[here, :]
+        hidden = silu(dot(own, weight(wr, 0)))
         branch = norm(dot(hidden, weight(wr, 1)), 2)
-        gout[here, :] = (cells.astype(F32) + branch).astype(BF16)
+        updated = (own.astype(F32) + branch).astype(BF16)
+        lines = C_STEP // grid_out.shape[1]
+        grid_out[pl.ds(step * lines, lines)] = updated.reshape(lines, *grid_out.shape[1:])
 
     loop(GRID // C_STEP, grid_step)
-    store_grid = pltpu.make_async_copy(gout, grid_out, store_sem.at[0])
-    store_grid.start()
     l_wn.wait()
 
     def out_first(step):
@@ -403,6 +408,16 @@
     total[...] = jnp.zeros((NODES, D), F32)
 
     far_base = NODES + NEAR_ROWS
+    last_base = NODES + NEAR_ROWS - LAST
+
+    def last_spots(step):
+        here = rows(step, P_STEP)
+        last_hot[here, :] = onehot(columns(P_POS, step, P_STEP), last_base, LAST)
+        sum_hot[:, pl.ds(pl.multiple_of(step * P_STEP, P_STEP), P_STEP)] = onehot_rows(
+            P_ROW, step, P_STEP
+        )
+
+    loop(P_EDGES // P_STEP, last_spots)
 
     def take(count, base, arrived):
         def step_of(step):
@@ -432,15 +447,15 @@
 
     loop(P_EDGES // P_STEP, project)
     last = near_part(NEAR_GROUPS[-1])
-    table[...] = dot(near_in[last, :], weight(wp, 1)).astype(BF16)
+    table[pl.ds(0, LAST), :] = dot(near_in[last, :], weight(wp, 1)).astype(BF16)
 
     def process_last(step):
         here = rows(step, P_STEP)
-        off = columns(P_POS, step, P_STEP)
-        hidden = silu(pre[here, :] + dot(onehot(off, NODES + last.start, last.size), table[...]))
+        hidden = silu(pre[here, :] + dot(last_hot[here, :], table[pl.ds(0, LAST), :]))
         branch = norm(dot(hidden, weight(wp, 3)), 3)
         updated = (pe[here, :].astype(F32) + branch).astype(BF16)
-        total[...] += dot(onehot_rows(P_ROW, step, P_STEP), updated)
+        hot = sum_hot[:, pl.ds(pl.multiple_of(step * P_STEP, P_STEP), P_STEP)]
+        total[...] += dot(hot, updated)
 
     loop(P_EDGES // P_STEP, process_last)
 
@@ -449,13 +464,9 @@
         summed = total[here, :].astype(BF16)
         hidden = silu(node_pre[here, :] + dot(summed, weight(wn, 1)))
         branch = norm(dot(hidden, weight(wn, 2)), 4)
-        mout[here, :] = (mid[here, :].astype(F32) + branch).astype(BF16)
+        mesh_out[here, :] = (mid[here, :].astype(F32) + branch).astype(BF16)
 
     loop(NODES // N_STEP, out_last)
-    store_mesh = pltpu.make_async_copy(mout, mesh_out, store_sem.at[1])
-    store_mesh.start()
-    store_mesh.wait()
-    store_grid.wait()
 
 
 def body(
@@ -476,11 +487,11 @@
     mesh_out, grid_out = pl.pallas_call(
         kernel,
         out_shape=(
-            jax.ShapeDtypeStruct((NODES, D), BF16),
-            jax.ShapeDtypeStruct((GRID, D), BF16),
+            pltpu.VMEM((NODES, D), BF16),
+            pltpu.VMEM(grid_nodes.shape, BF16),
         ),
         in_specs=[smem, smem] + [any_space] * 16,
-        out_specs=(any_space, any_space),
+        out_specs=(pl.BlockSpec(memory_space=pltpu.VMEM), pl.BlockSpec(memory_space=pltpu.VMEM)),
         scratch_shapes=[
             ints(G_BLOCKS, 128), ints(G_BLOCKS, 128), ints(P_BLOCKS, 128), ints(P_BLOCKS, 128),
             ints(9, 1, NCAP), ints(1, FAR, DEVICES), pltpu.VMEM((5, 2, D), F32), ints(64, 128),
@@ -488,12 +499,13 @@
             buf(4 * D), buf(3 * D), buf(2 * D), buf(4 * D), buf(3 * D),
             buf(P_EDGES, F32), buf(P_EDGES), buf(NODES, F32), buf(NODES, F32), buf(NODES),
             buf(NEAR_ROWS), buf(NEAR_ROWS), buf(DEVICES * FAR), buf(DEVICES * FAR),
-            buf(GRID), buf(NODES), buf(DEVICES * FAR), buf(HALO_PAD),
-            dma((16,)), dma((2,)), dma((8,)), dma((8,)), dma((8,)), dma((8,)),
+            buf(DEVICES * FAR), buf(HALO_PAD), buf(GRID),
+            pltpu.VMEM((P_EDGES, LAST), BF16), pltpu.VMEM((NODES, P_EDGES), BF16),
+            dma((16,)), dma((8,)), dma((8,)), dma((8,)), dma((8,)),
             dma((FAR_GROUPS,)), dma((FAR_GROUPS,)), pltpu.SemaphoreType.REGULAR,
         ],
         compiler_params=pltpu.CompilerParams(
-            collective_id=0, has_side_effects=True, vmem_limit_bytes=63 * 2**20
+            collective_id=0, has_side_effects=True, vmem_limit_bytes=60 * 2**20
         ),
     )(
         g2m_window, mesh_window,
@@ -502,7 +514,7 @@
         w_g2m_edge.reshape(-1, D), w_mesh_node.reshape(-1, D), w_grid_node.reshape(-1, D),
         w_proc_edge.reshape(-1, D), w_proc_node.reshape(-1, D),
     )
-    return mesh_out, grid_out.reshape(grid_nodes.shape)
+    return mesh_out, grid_out
 
 
 def solution(mesh):

time: 78.7 us -> 71.6 us (0.910)
  Pallas kernels: 73.7 us -> 69 us
  local copies, waits for them, and re-layouts: 4.16 us -> 1.77 us
    pallas_call x1, Pallas kernels: 73.7 us -> 69 us  [body(): pl.pallas_call(kernel, out_shape=(pltpu.VMEM((NODES, D), BF16), pltpu.VME...]
    unnamed x2, local copies, waits for them, and re-layouts: 4.16 us -> 1.77 us
where the time goes in v3:
time: 71.6 us; the launch traced here: 71.4 us
  Pallas kernels  69 us (96%)
  local copies, waits for them, and re-layouts  1.77 us (2%)
    pallas_call x1, Pallas kernels, body(): pl.pallas_call(kernel, out_shape=(pltpu.VMEM((NODES, D), BF16), pltpu.VME...  69 us
    unnamed x2, local copies, waits for them, and re-layouts  1.77 us

profile of v3, /device:TPU:1, one launch (start us, length us, event | category | flops | bytes accessed | tf_op | source)
XLA Modules:
  0.0 71.4 jit_solution(15758105412836165601)
XLA Ops:
  0.6 69.0 %shard_map.185 = (bf16[512,512]{1,0:T(8,128)(2,1)S(1)}, bf16[16,64,512]{2,1,0:T(8,128)(2,1)S(1)}) custom-call(s32[14]{0:T(128)} %g_window.1, s32[16]{0:T(128)} %p_window.1, s32[14,128]{1,0:T(8,128)} %gs_h.1, s32[14,128]{1,0:T(8,128)} %gr_h.1, s32[16,128]{1,0:T(8,128)} %ps_h.1, s32[16,128]{1,0:T(8,128)} %pr_h.1, s32[9,1,192]{2,1,0:T(1,128)} %bitcast.18, ...), custom_call_target="tpu_custom_call" | custom-call | tf_op jit(solution)/shard_map/pallas_call | solution.py:487
  69.7 0.8 %copy.22 = bf16[512,512]{1,0:T(8,128)(2,1)} copy(bf16[512,512]{1,0:T(8,128)(2,1)S(1)} %get-tuple-element.2) | data formatting | bytes 1048576
  70.5 1.0 %copy.23 = bf16[16,64,512]{2,1,0:T(8,128)(2,1)} copy(bf16[16,64,512]{2,1,0:T(8,128)(2,1)S(1)} %get-tuple-element.3) | data formatting | bytes 2097152

commit v4 on v3

--- a/solution.py
+++ b/solution.py
@@ -20,7 +20,7 @@
 NEAR = 9 * NCAP
 NEAR_ORDER = (1, 7, 3, 5, 0, 2, 6, 8)
 NEAR_ROWS = 8 * NCAP
-NEAR_GROUPS = ((0, 2), (2, 6), (6, 8))
+NEAR_GROUPS = ((0, 2), (2, 4), (4, 8))
 LAST = (NEAR_GROUPS[-1][1] - NEAR_GROUPS[-1][0]) * NCAP
 FAR = 16
 DEVICES = 128
@@ -42,14 +42,14 @@
 HOPS = 10
 
 SEGMENTS = (
-    (1, 0, 0, 256),
-    (-1, 0, 256, 256),
     (0, 1, 512, 64),
     (0, -1, 576, 64),
     (1, 1, 640, 16),
     (1, -1, 656, 16),
     (-1, 1, 672, 16),
     (-1, -1, 688, 16),
+    (1, 0, 0, 256),
+    (-1, 0, 256, 256),
 )
 
 
@@ -198,10 +198,10 @@
     strips[...] = dot(jnp.where(cell == wanted, 1.0, 0.0).astype(BF16), grid[...]).astype(BF16)
 
     sources = (
-        grid.at[pl.ds(768, 256)], grid.at[pl.ds(0, 256)],
         strips.at[pl.ds(64, 64)], strips.at[pl.ds(0, 64)],
         strips.at[pl.ds(112, 16)], strips.at[pl.ds(48, 16)],
         strips.at[pl.ds(64, 16)], strips.at[pl.ds(0, 16)],
+        grid.at[pl.ds(768, 256)], grid.at[pl.ds(0, 256)],
     )
     pl.semaphore_wait(barrier, len(SEGMENTS) + len(steps_back))
     halo_copies = [
@@ -251,25 +251,23 @@
 
     edge = lax.broadcasted_iota(jnp.int32, (F_STEP, DEVICES), 0)
     lane_of = lax.broadcasted_iota(jnp.int32, (F_STEP, DEVICES), 1)
-    of_slot = jnp.where(
-        (lax.broadcasted_iota(jnp.int32, (F_STEP, FAR), 0) & (FAR - 1))
-        == lax.broadcasted_iota(jnp.int32, (F_STEP, FAR), 1), 1.0, 0.0
+    part = lax.broadcasted_iota(jnp.int32, (F_STEP, 2 * FAR), 1)
+    of_slot = (
+        (lax.broadcasted_iota(jnp.int32, (F_STEP, 2 * FAR), 0) & (FAR - 1)) == (part & (FAR - 1))
     )
-    spread = jnp.ones((FAR, 128), BF16)
+    spread = jnp.where(
+        lax.broadcasted_iota(jnp.int32, (2 * FAR, 128), 0) < FAR, 16.0, 1.0
+    ).astype(BF16)
+    lists = jnp.concatenate([far[0] >> 4, far[0] & 15], axis=0).astype(F32).astype(BF16)
 
     def far_spots(step):
         place = (edge >> 4) + step * (F_STEP // FAR)
         of_list = jnp.where(((me + place * FAR_MUL) & (DEVICES - 1)) == lane_of, 1.0, 0.0).astype(BF16)
-
-        def expand(part):
-            mine = lax.dot_general(
-                of_list, part.astype(F32).astype(BF16), (((1,), (1,)), ((), ())),
-                preferred_element_type=F32,
-            )
-            return dot((mine * of_slot).astype(BF16), spread)
-
-        lists = far[0]
-        off = 16.0 * expand(lists >> 4) + expand(lists & 15) - lane_of.astype(F32)
+        mine = lax.dot_general(
+            of_list, lists, (((1,), (1,)), ((), ())), preferred_element_type=F32
+        )
+        node = dot(jnp.where(of_slot, mine, 0.0).astype(BF16), spread)
+        off = node - lane_of.astype(F32)
         far_hot[rows(step, F_STEP), :] = jnp.concatenate(
             [jnp.where(off == 128.0 * k, 1.0, 0.0).astype(BF16) for k in range(NODES // 128)], axis=1
         )
@@ -282,7 +280,6 @@
         node_pre[here, :] = dot(mesh[here, :], weight(wm, 0))
 
     loop(NODES // N_STEP, node_first)
-    total[...] = jnp.zeros((NODES, D), F32)
     for copy in halo_copies:
         copy.wait()
 
@@ -294,9 +291,9 @@
         hidden = silu(pre[here, :] + dot(onehot(pos, GRID, HALO_PAD), table[pl.ds(0, HALO_PAD), :]))
         branch = norm(dot(hidden, weight(wg, 3)), 0)
         updated = (ge[here, :].astype(F32) + branch).astype(BF16)
-        total[...] += dot(onehot_rows(G_ROW, step, E_STEP), updated)
-
-    loop(G_EDGES // E_STEP, encode_last)
+        total[...] = dot(onehot_rows(G_ROW, step, E_STEP), updated)
+
+    encode_last(0)
 
     def node_last(step):
         here = rows(step, N_STEP)
@@ -405,7 +402,6 @@
         node_pre[here, :] = dot(mid[here, :], weight(wn, 0))
 
     loop(NODES // N_STEP, out_first)
-    total[...] = jnp.zeros((NODES, D), F32)
 
     far_base = NODES + NEAR_ROWS
     last_base = NODES + NEAR_ROWS - LAST
@@ -455,9 +451,9 @@
         branch = norm(dot(hidden, weight(wp, 3)), 3)
         updated = (pe[here, :].astype(F32) + branch).astype(BF16)
         hot = sum_hot[:, pl.ds(pl.multiple_of(step * P_STEP, P_STEP), P_STEP)]
-        total[...] += dot(hot, updated)
-
-    loop(P_EDGES // P_STEP, process_last)
+        total[...] = dot(hot, updated)
+
+    process_last(0)
 
     def out_last(step):
         here = rows(step, N_STEP)

time: 71.6 us -> 71.1 us (level)
  no operation moved by 1% of the time
where the time goes in v4:
time: 71.1 us; the launch traced here: 71 us
  Pallas kernels  68.6 us (96%)
  local copies, waits for them, and re-layouts  1.77 us (2%)
    pallas_call x1, Pallas kernels, body(): pl.pallas_call(kernel, out_shape=(pltpu.VMEM((NODES, D), BF16), pltpu.VME...  68.6 us
    unnamed x2, local copies, waits for them, and re-layouts  1.77 us

profile of v4, /device:TPU:1, one launch (start us, length us, event | category | flops | bytes accessed | tf_op | source)
XLA Modules:
  0.0 71.0 jit_solution(4577276333189784316)
XLA Ops:
  0.6 68.6 %shard_map.185 = (bf16[512,512]{1,0:T(8,128)(2,1)S(1)}, bf16[16,64,512]{2,1,0:T(8,128)(2,1)S(1)}) custom-call(s32[14]{0:T(128)} %g_window.1, s32[16]{0:T(128)} %p_window.1, s32[14,128]{1,0:T(8,128)} %gs_h.1, s32[14,128]{1,0:T(8,128)} %gr_h.1, s32[16,128]{1,0:T(8,128)} %ps_h.1, s32[16,128]{1,0:T(8,128)} %pr_h.1, s32[9,1,192]{2,1,0:T(1,128)} %bitcast.18, ...), custom_call_target="tpu_custom_call" | custom-call | tf_op jit(solution)/shard_map/pallas_call | solution.py:483
  69.3 0.8 %copy.22 = bf16[512,512]{1,0:T(8,128)(2,1)} copy(bf16[512,512]{1,0:T(8,128)(2,1)S(1)} %get-tuple-element.2) | data formatting | bytes 1048576
  70.1 1.0 %copy.23 = bf16[16,64,512]{2,1,0:T(8,128)(2,1)} copy(bf16[16,64,512]{2,1,0:T(8,128)(2,1)S(1)} %get-tuple-element.3) | data formatting | bytes 2097152
